TPU v7x, 32 devices: a whole 2x2x4 slice. The times are simulated.
32 devices in a mesh: dp: 2 (over x), head: 1, row: 16 (over z, y, core).
Axes of the slice: x: 2, y: 2, z: 4, core: 2. Of those that a mesh axis runs over, the one named last changes fastest.
Arguments:
- pair_act: bfloat16 [256, 128, 128], P(('dp', 'row')), parts along dimension 0, may hold values from -12 to 12
- chain_id: int32 [256], P('dp'), parts along dimension 0, may hold values from 0 to 3, never falling along the last dimension, each value on 1 to 64 neighbouring positions
- residue_mask: int32 [256], P('dp'), parts along dimension 0, may hold values 0 or 1
- norm_gain: float32 [128], replicated, may hold values from 0.5 to 1.5
- w_proj: bfloat16 [128, 4, 128], P(None, 'head'), may hold values from -1.25 to 1.25
- w_bias: bfloat16 [128, 4], P(None, 'head'), may hold values from -0.9 to 0.9
- chain_bias: float32 [2, 4], P(None, 'head'), may hold values from -2 to 2
- w_out: bfloat16 [4, 32, 128], P('head'), may hold values from -0.5 to 0.5
- w_dist: bfloat16 [128, 64], replicated, may hold values from -0.5 to 0.5
- dist_bias: float32 [64], replicated, may hold values from -3 to 3
Outputs:
- new_pair: bfloat16 [256, 128, 128], P(('dp', 'row')), parts along dimension 0
- distogram: bfloat16 [256, 128, 64], P(('dp', 'row')), parts along dimension 0
There are 2 independent parts, one for each index of `dp`. A program takes and returns all parts, laid end to end along the dimension named above; an argument that names none is the same for every part. Nothing has to cross between parts.
Inputs may be any that keep to these rules, and one draw needn't show every extreme that they name: `chain_id`: chain ids never fall along the residues; no chain has more than half of the 128 residues.
All inputs are finite; a program needn't handle non-finite values.
Results may differ from a plain program's by a relative error of at most 0.013.
Values may be sent and summed in bfloat16 or wider, within the bound.
No kernel may reach another device: no remote copies, remote signals or barrier semaphores. Data moves between devices by JAX's collectives and lax.ppermute only.
A program may use at most 64 MiB of HBM per device.

v0:
```python
import functools

import jax
import jax.numpy as jnp
from jax import lax
from jax.experimental import pallas as pl
from jax.experimental.pallas import tpu as pltpu
from jax.sharding import PartitionSpec as P

LANES = 128
F32 = jnp.float32
BF16 = jnp.bfloat16
LOG2E = 1.4426950408889634


def dot_nt(a, b):
    return lax.dot_general(a, b, (((1,), (1,)), ((), ())), preferred_element_type=F32)


def dot_tn(a, b):
    return lax.dot_general(a, b, (((0,), (0,)), ((), ())), preferred_element_type=F32)


def dot_nn(a, b):
    return jnp.dot(a, b, preferred_element_type=F32)


def layer_norm(values, gain):
    center = jnp.mean(values, -1, keepdims=True)
    centered = values - center
    variance = jnp.mean(centered * centered, -1, keepdims=True)
    return (centered * lax.rsqrt(variance + 1e-05) * gain).astype(BF16)


def swap_matrix(rows):
    size = 2 * rows * rows
    out = lax.broadcasted_iota(jnp.int32, (size, size), 0)
    col = lax.broadcasted_iota(jnp.int32, (size, size), 1)
    b, rest = out // (2 * rows), out % (2 * rows)
    wanted = (rest // rows) * (rows * rows) + (rest % rows) * rows + b
    return jnp.where(col == wanted, 1.0, 0.0).astype(BF16)


def pack_kernel(x_hbm, gain_hbm, wb_hbm, out_hbm, x_ref, gain_ref, wb_ref, out_ref, sems, out_sems):
    rows, n, chan = x_ref.shape
    peers = n // rows
    heads = wb_ref.shape[0]
    half = heads * rows // 2
    base = rows * rows
    fetch_gain = pltpu.make_async_copy(gain_hbm, gain_ref, sems.at[rows])
    fetch_wb = pltpu.make_async_copy(wb_hbm, wb_ref, sems.at[rows + 1])
    fetches = [pltpu.make_async_copy(x_hbm.at[k], x_ref.at[k], sems.at[k]) for k in range(rows)]
    for copy in (fetch_gain, fetch_wb, *fetches):
        copy.start()
    stores = []

    def store(first, count):
        at = pl.ds(first, count)
        copy = pltpu.make_async_copy(out_ref.at[:, at, :], out_hbm.at[:, at, :], out_sems.at[len(stores)])
        copy.start()
        stores.append(copy)

    owner = lax.broadcasted_iota(jnp.int32, (heads * rows, chan), 0) % rows
    bias = jnp.zeros((heads * rows, n), F32)
    fetch_gain.wait()
    fetch_wb.wait()
    gain = gain_ref[...]
    wb = wb_ref[...].astype(F32)
    wb = jnp.concatenate([jnp.broadcast_to(wb[h : h + 1], (rows, chan)) for h in range(heads)], 0)
    mine = [jnp.where(owner == k, wb, 0.0).astype(BF16) for k in range(rows)]
    mine = [jnp.concatenate(mine[k : k + 2], 1) for k in range(0, rows, 2)]
    for copy in fetches:
        copy.wait()
    for pair in range(rows // 2):
        both = [x_ref[k].astype(F32).reshape(peers, rows, chan) for k in (2 * pair, 2 * pair + 1)]
        out_ref[:, 2 * rows * pair : 2 * rows * (pair + 1), :] = jnp.concatenate(both, 1).astype(BF16)
    store(0, base)
    normed = [layer_norm(x_ref[k].astype(F32), gain) for k in range(rows)]
    for pair in range(rows // 2):
        bias = bias + dot_nt(mine[pair], jnp.concatenate(normed[2 * pair : 2 * pair + 2], 1))
    bias = bias.astype(BF16)
    for t in range(n // LANES):
        block = bias[:, t * LANES : (t + 1) * LANES]
        for d in range(peers):
            part = block[(d % 2) * half : (d % 2 + 1) * half]
            out_ref[d, base + t * half : base + (t + 1) * half] = part
    store(base, (n // LANES) * half)
    for copy in stores:
        copy.wait()


def prepare_kernel(
    heads, rows,
    chain_ref, mask_ref, cb_ref, w_ref, db_ref, gain_ref, wo_ref, wd_ref,
    term_ref, wt_ref, wk_out, dbc_ref, gain_out, wo_out, wd_out, swap_ref,
):
    gain_out[...] = gain_ref[...]
    swap_ref[...] = swap_matrix(rows)
    chan = w_ref.shape[0]
    width = wo_ref.shape[0]
    half = heads // 2
    core = lax.axis_index("row") % 2
    w_out = wo_ref[...].astype(F32)
    other_first = jnp.concatenate([w_out[width // 2 :], w_out[: width // 2]], 0)
    w_out = jnp.where(core == 0, w_out, other_first).astype(BF16)
    wk_out[...] = jnp.zeros_like(wk_out)
    wo_out[...] = jnp.zeros_like(wo_out)
    for side in range(2):
        wo_out[side * width : (side + 1) * width, side * chan : (side + 1) * chan] = w_out
    wd_out[...] = wd_ref[...]
    n = chain_ref.shape[1]
    tiles = n // LANES
    dim = w_ref.shape[2] // 4

    def column_of(row):
        return jnp.transpose(jnp.broadcast_to(row, (LANES, LANES)))

    for kt in range(tiles):
        ks = slice(kt * LANES, (kt + 1) * LANES)
        chain_k = column_of(chain_ref[:, ks].astype(F32))
        mask_k = (column_of(mask_ref[:, ks].astype(F32)) - 1.0) * 1000000000.0
        for it in range(tiles):
            cs = slice(it * LANES, (it + 1) * LANES)
            same = chain_k == chain_ref[:, cs].astype(F32)
            for h in range(heads):
                inside, outside = [jnp.where(core == 0, cb_ref[r, h], cb_ref[r, (h + half) % heads]) for r in (1, 0)]
                term_ref[h, ks, cs] = (jnp.where(same, inside, outside) + mask_k) * LOG2E
    for h in range(heads):
        mine = jnp.where(core == 0, w_ref[:, h, :].astype(F32), w_ref[:, (h + half) % heads, :].astype(F32))
        turned = jnp.transpose(mine).astype(BF16)
        for place, kind in enumerate((0, 2, 3)):
            start = place * width + h * dim
            wt_ref[start : start + dim] = turned[kind * dim : (kind + 1) * dim]
        for side in range(2):
            start = side * width + h * dim
            wk_out[start : start + dim, side * chan : (side + 1) * chan] = turned[dim : 2 * dim]
    bins = dbc_ref.shape[0]
    db_rows = jnp.broadcast_to(jnp.concatenate([db_ref[...], db_ref[...]], 1)[:, :LANES], (LANES, LANES))
    dbc_ref[...] = jnp.transpose(db_rows)[:bins]


def unpack_bias(blocks, term_ref, first, bias_ref):
    half, n = bias_ref.shape[0], bias_ref.shape[1]
    rows = n // len(blocks)
    for s, block in enumerate(blocks):
        at = slice(s * rows, (s + 1) * rows)
        extra = block.astype(F32) * LOG2E
        for t in range(n // LANES):
            cs = slice(t * LANES, (t + 1) * LANES)
            for h in range(half):
                start = (t * half + h) * rows
                bias_ref[h, at, cs] = extra[start : start + rows] + term_ref[first + h, at, cs]


def soften(j, t, keys, spread, bias_ref, scaling, inv_s, e_s):
    scores = dot_nn(keys, spread)
    for h in range(bias_ref.shape[0]):
        cs = slice(h * LANES, (h + 1) * LANES)
        s = scores[:, cs] * scaling + bias_ref[h, :, t * LANES : (t + 1) * LANES]
        e = jnp.exp2(s - jnp.max(s, 0, keepdims=True))
        inv_s[j, t, h : h + 1] = 1.0 / jnp.sum(e, 0, keepdims=True)
        e_s[j, t, :, cs] = e.astype(BF16)


def combine(j, t, values, gates, inv_s, e_s, gated_ref):
    half = inv_s.shape[2]
    dim = values.shape[0] // half
    cs = slice(t * LANES, (t + 1) * LANES)
    o = dot_nn(values, e_s[j, t])
    for h in range(half):
        mine = slice(h * dim, (h + 1) * dim)
        part = o[mine, h * LANES : (h + 1) * LANES] * inv_s[j, t, h : h + 1]
        gated_ref[j, mine, cs] = (gates[mine, cs] * part).astype(BF16)


def for_each(count, tiles, body):
    if tiles == 1:
        for i in range(count):
            body(i)
    else:

        @pl.loop(0, count)
        def _(i):
            body(i)


def permuted(blocks, swap):
    left, right = jnp.concatenate(blocks[:2], 0), jnp.concatenate(blocks[2:], 0)
    return dot_nn(swap, jnp.concatenate([left, right], 1))


def project_kernel(
    heads,
    recv_ref, gain_ref, w_ref, wk_ref, swap_ref, term_ref,
    x_s, spread_s, k_s, v_s, g_s, gated_ref,
    n_s, own_spread, own_v, own_g, bias_s, inv_s, e_s,
):
    peers = recv_ref.shape[0]
    rows, n, chan = x_s.shape
    tiles = n // LANES
    dim = w_ref.shape[0] // (3 * heads)
    width = heads * dim
    base = rows * rows
    gain = gain_ref[...]
    swap = swap_ref[...]
    group = 2 * rows
    w_k = wk_ref[...]

    quads = range(peers // 4)
    x = [permuted([recv_ref[4 * quad + s, :base] for s in range(4)], swap) for quad in quads]
    normed = [[layer_norm(two[:, :chan], gain), layer_norm(two[:, chan:], gain)] for two in x]
    keys = [dot_nt(jnp.concatenate(two, 1), w_k).astype(BF16) for two in normed]
    for quad in quads:
        for side in range(2):
            at = slice((2 * quad + side) * group, (2 * quad + side + 1) * group)
            x_s[:, at, :] = x[quad][:, side * chan : (side + 1) * chan].astype(BF16).reshape(rows, group, chan)
            n_s[:, at, :] = normed[quad][side].reshape(rows, group, chan)
            k_s[:, at, :] = keys[quad][:, side * width : (side + 1) * width].reshape(rows, group, width)

    half, part = heads // 2, width // 2
    unpack_bias([recv_ref[s, base:] for s in range(peers)], term_ref, 0, bias_s)
    w_qvg = w_ref[...]
    zero = jnp.zeros((dim, LANES), BF16)

    def project(pair):
        both = dot_nt(w_qvg, n_s[pl.ds(2 * pair, 2)].reshape(2 * n, chan)).astype(BF16)
        for side in range(2):
            j = 2 * pair + side
            qvg = both[:, side * n : (side + 1) * n]
            gate = jax.nn.sigmoid(qvg[2 * width :].astype(F32))
            own_v[j], v_s[j] = qvg[width : width + part], qvg[width + part : 2 * width]
            own_g[j], g_s[j] = gate[:part], gate[part:]
            for t in range(tiles):
                for h in range(heads):
                    target = (own_spread, spread_s)[h // half]
                    cs = slice(h % half * LANES, (h % half + 1) * LANES)
                    for other in range(heads):
                        block = qvg[h * dim : (h + 1) * dim, t * LANES : (t + 1) * LANES] if h == other else zero
                        target[j, t, other * dim : (other + 1) * dim, cs] = block

    scaling = dim ** (-0.5) * LOG2E
    for_each(rows // 2, tiles, project)
    for_each(rows, tiles, lambda j: [soften(j, t, k_s[j], own_spread[j, t], bias_s, scaling, inv_s, e_s) for t in range(tiles)])
    for_each(rows, tiles, lambda j: [combine(j, t, own_v[j], own_g[j], inv_s, e_s, gated_ref) for t in range(tiles)])


def attend_kernel(
    fused,
    other_ref, term_ref, wo_ref, wd_ref, db_ref, x_s, spread_s, k_s, v_s, g_s, gated_ref,
    out_ref, *refs,
):
    if fused:
        second_ref, bias_s, inv_s, e_s, gated_s, new_s = refs
    else:
        bias_s, inv_s, e_s, gated_s = refs
    peers = other_ref.shape[0]
    rows, n, chan = x_s.shape
    tiles = n // LANES
    half, part = bias_s.shape[0], v_s.shape[1]
    scaling = (part // half) ** (-0.5) * LOG2E
    w_out = wo_ref[...]

    unpack_bias([other_ref[s] for s in range(peers)], term_ref, half, bias_s)
    for_each(rows, tiles, lambda j: [soften(j, t, k_s[j], spread_s[j, t], bias_s, scaling, inv_s, e_s) for t in range(tiles)])
    for_each(rows, tiles, lambda j: [combine(j, t, v_s[j], g_s[j], inv_s, e_s, gated_s) for t in range(tiles)])

    def updated(pair):
        both = [ref[2 * pair + side] for side in range(2) for ref in (gated_ref, gated_s)]
        return dot_tn(jnp.concatenate(both, 0), w_out).astype(BF16)

    def store_update(pair):
        update = updated(pair)
        for side in range(2):
            out_ref[2 * pair + side] = update[:, side * chan : (side + 1) * chan]

    if not fused:
        for_each(rows // 2, tiles, store_update)
        return

    for j in range(0, rows, 2):
        update = updated(j // 2).astype(F32)
        both = []
        for side in range(2):
            new = (x_s[j + side].astype(F32) + update[:, side * chan : (side + 1) * chan]).astype(BF16)
            new_s[j + side] = new
            both.append(new.astype(F32).reshape(peers, rows, chan))
        out_ref[:, j * rows : (j + 2) * rows, :] = jnp.concatenate(both, 1).astype(BF16)
    logits_of(new_s, wd_ref[...], db_ref[:, :1], second_ref)


def logits_of(new_ref, w_dist, d_bias, out_ref):
    rows, n, chan = new_ref.shape
    logits = dot_nt(w_dist, new_ref[...].reshape(rows * n, chan)) + d_bias
    for j in range(rows):
        out_ref[j] = logits[:, j * n : (j + 1) * n].astype(BF16)


def finish_kernel(recv_ref, mirror_ref, wd_ref, db_ref, swap_ref, new_hbm, dist_hbm, new_ref, dist_ref, sems):
    peers, _, chan = recv_ref.shape
    rows = new_ref.shape[0]
    group = 2 * rows
    swap = swap_ref[...]
    for quad in range(peers // 4):
        new = permuted([recv_ref[4 * quad + s] for s in range(4)], swap).astype(BF16)
        for side in range(2):
            at = slice((2 * quad + side) * group, (2 * quad + side + 1) * group)
            new_ref[:, at, :] = new[:, side * chan : (side + 1) * chan].reshape(rows, group, chan)
    copies = [pltpu.make_async_copy(new_ref, new_hbm, sems.at[0])]
    copies[0].start()
    logits_of(new_ref, wd_ref[...], db_ref[:, :1], dist_ref)
    for i in range(rows):
        dist_ref[i] = (dist_ref[i].astype(F32) + mirror_ref[i].astype(F32)).astype(BF16)
        if i % 2:
            at = pl.ds(i - 1, 2)
            copies.append(pltpu.make_async_copy(dist_ref.at[at], dist_hbm.at[at], sems.at[1 + i // 2]))
            copies[-1].start()
    for copy in copies:
        copy.wait()


def call(kernel, outs, args, scratch=(), smem=(), hbm=(), hbm_outs=False, limit=48):
    spaces = [pltpu.SMEM if i in smem else pl.ANY if i in hbm else pltpu.VMEM for i in range(len(args))]
    return pl.pallas_call(
        kernel,
        out_shape=[jax.ShapeDtypeStruct(s, d) for s, d in outs],
        in_specs=[pl.BlockSpec(memory_space=space) for space in spaces],
        out_specs=[pl.BlockSpec(memory_space=pl.ANY if hbm_outs else pltpu.VMEM)] * len(outs),
        scratch_shapes=list(scratch),
        compiler_params=pltpu.CompilerParams(vmem_limit_bytes=limit * 1024 * 1024),
    )(*args)


def swap_cores(values):
    peers = lax.axis_size("row")
    return lax.ppermute(values, "row", [(i, i ^ 1) for i in range(peers)])


def all_to_all(blocks):
    return lax.all_to_all(blocks, "row", split_axis=0, concat_axis=0, tiled=True)


def shards(
    pair_act, chain_id, residue_mask, norm_gain, w_proj, w_bias, chain_bias, w_out, w_dist, dist_bias,
):
    rows, n, chan = pair_act.shape
    peers = n // rows
    heads, dim = w_out.shape[0], w_out.shape[1]
    bins = w_dist.shape[1]
    tiles = n // LANES
    width = heads * dim
    fused = lax.axis_size("head") == 1
    gain = norm_gain[None, :]
    base = rows * rows
    length = base + tiles * heads * rows // 2

    (packed,) = call(
        pack_kernel,
        [((peers, length, chan), BF16)],
        [pair_act, gain, w_bias.T],
        scratch=[
            pltpu.VMEM(pair_act.shape, BF16),
            pltpu.VMEM(gain.shape, F32),
            pltpu.VMEM((heads, chan), BF16),
            pltpu.VMEM((peers, length, chan), BF16),
            pltpu.SemaphoreType.DMA((rows + 2,)),
            pltpu.SemaphoreType.DMA((2,)),
        ],
        hbm=(0, 1, 2),
        hbm_outs=True,
        limit=60,
    )
    received = all_to_all(packed)
    prepared = call(
        functools.partial(prepare_kernel, heads, rows),
        [
            ((heads, n, n), F32), ((3 * width, chan), BF16), ((2 * width, 2 * chan), BF16), ((bins, LANES), F32),
            ((1, chan), F32), ((2 * width, 2 * chan), BF16), ((bins, chan), BF16),
            ((2 * base, 2 * base), BF16),
        ],
        [
            chain_id[None, :], residue_mask[None, :], chain_bias, w_proj, dist_bias[None, :],
            gain, w_out.reshape(width, chan), w_dist.T,
        ],
        smem=(2,),
    )
    received, *prepared = lax.optimization_barrier((received, *prepared))
    term, w_types, w_keys, db_col, gain, w_out, wd_t, swap = prepared
    other_bias = swap_cores(received[:, base:])
    spread_shape = ((rows, tiles, width, heads // 2 * LANES), BF16)
    values_shape, gates_shape = ((rows, width // 2, n), BF16), ((rows, width // 2, n), F32)
    softmax_scratch = [
        pltpu.VMEM((heads // 2, n, n), F32),
        pltpu.VMEM((rows, tiles, heads // 2, LANES), F32),
        pltpu.VMEM((rows, tiles, n, heads // 2 * LANES), BF16),
    ]
    x_cols, spread, keys, values, gates, gated = call(
        functools.partial(project_kernel, heads),
        [
            ((rows, n, chan), BF16),
            spread_shape,
            ((rows, n, width), BF16),
            values_shape,
            gates_shape,
            values_shape,
        ],
        [received, gain, w_types, w_keys, swap, term],
        scratch=[
            pltpu.VMEM((rows, n, chan), BF16),
            *(pltpu.VMEM(*shape) for shape in (spread_shape, values_shape, gates_shape)),
            *softmax_scratch,
        ],
    )
    if fused:
        outs = [((peers, base, chan), BF16), ((rows, bins, n), BF16)]
    else:
        outs = [((rows, n, chan), BF16)]
    result = call(
        functools.partial(attend_kernel, fused),
        outs,
        [other_bias, term, w_out, wd_t, db_col, x_cols, spread, keys, values, gates, gated],
        scratch=softmax_scratch + [pltpu.VMEM(*values_shape)] + [pltpu.VMEM((rows, n, chan), BF16)] * fused,
    )
    if fused:
        to_rows, mirror = result
    else:
        update = lax.psum(result[0], "head").astype(F32)
        new = (x_cols.astype(F32) + update).astype(BF16)
        logits = jnp.einsum("cb,jic->jbi", w_dist, new, preferred_element_type=F32)
        mirror = (logits + dist_bias[None, :, None]).astype(BF16)
        to_rows = new.reshape(rows, peers, rows, chan).transpose(1, 0, 2, 3).reshape(peers, base, chan)
    arrived = all_to_all(to_rows)
    new_rows, dist = call(
        finish_kernel,
        [((rows, n, chan), BF16), ((rows, bins, n), BF16)],
        [arrived, mirror, wd_t, db_col, swap],
        scratch=[
            pltpu.VMEM((rows, n, chan), BF16),
            pltpu.VMEM((rows, bins, n), BF16),
            pltpu.SemaphoreType.DMA((1 + rows // 2,)),
        ],
        hbm_outs=True,
    )
    return new_rows, dist.transpose(0, 2, 1)


def solution(mesh):
    in_specs = (
        P(("dp", "row"), None, None),
        P("dp"),
        P("dp"),
        P(),
        P(None, "head", None),
        P(None, "head"),
        P(None, "head"),
        P("head", None, None),
        P(),
        P(),
    )
    out_specs = (P(("dp", "row"), None, None), P(("dp", "row"), None, None))
    return jax.shard_map(shards, mesh=mesh, in_specs=in_specs, out_specs=out_specs, check_vma=False)
```

profile of v0, /device:TPU:0, one launch (start us, length us, event | category | flops | bytes accessed | tf_op | source)
XLA Modules:
  0.0 38.5 jit_solution(4758460875607506367)
XLA Ops:
  0.6 2.1 %shard_map.113 = bf16[16,80,128]{2,1,0:T(8,128)(2,1)} custom-call(bf16[8,128,128]{2,1,0:T(8,128)(2,1)} %x_hbm.1, f32[1,128]{1,0:T(1,128)} %bitcast.10, bf16[4,128]{1,0:T(4,128)(2,1)} %bitcast.15), custom_call_target="tpu_custom_call" | custom-call | tf_op jit(solution)/shard_map/pallas_call | solution.py:323
  2.8 0.0 copy-start
  2.8 0.0 copy-start.1
  2.8 0.0 copy-start.2
  2.8 0.0 copy-start.5
  2.8 0.0 copy-start.6
  2.8 0.0 copy-start.7
  2.8 7.5 %all-to-all-start = ((bf16[16,80,128]{2,1,0:T(8,128)(2,1)}), bf16[16,80,128]{2,1,0:T(8,128)(2,1)S(1)}, u32[]{:S(2)}, u32[]{:S(2)}) async-start(bf16[16,80,128]{2,1,0:T(8,128)(2,1)} %shard_map.113), calls=%async_computation | async-start | bytes 655360 | tf_op jit(solution)/shard_map/all_to_all | solution.py:339
  10.4 0.0 copy-start.3
  10.4 0.0 copy-start.4
  10.4 0.0 copy-done
  10.4 0.0 copy-done.1
  10.4 0.0 copy-done.2
  10.4 0.0 copy-done.5
  10.5 0.6 %copy-done.3 = f32[128]{0:T(128)S(1)} copy-done((f32[128]{0:T(128)S(1)}, f32[128]{0:T(128)}, u32[]{:S(2)}) %copy-start.3) | copy-done | bytes 536
  11.0 0.0 copy-done.4
  11.1 1.0 %shard_map.114 = (f32[4,128,128]{2,1,0:T(8,128)S(1)}, bf16[384,128]{1,0:T(8,128)(2,1)S(1)}, bf16[256,256]{1,0:T(8,128)(2,1)S(1)}, f32[64,128]{1,0:T(8,128)S(1)},...) custom-call(s32[1,128]{1,0:T(1,128)S(1)} %bitcast.12, ...), custom_call_target="tpu_custom_call" | custom-call | tf_op jit(solution)/shard_map/pallas_call | solution.py:323
  12.1 9.4 %all-to-all-done.recv_ref = bf16[16,80,128]{2,1,0:T(8,128)(2,1)S(1)} async-done(((bf16[16,80,128]{2,1,0:T(8,128)(2,1)}), bf16[16,80,128]{2,1,0:T(8,128)(2,1)S(1)}, u32[]{:S(2)}, u32[]{:S(2)}) %all-to-all-start) | async-done | bytes 327712 | tf_op jit(solution)/shard_map/all_to_all | solution.py:339
  21.5 0.1 collective-permute-start
  21.6 1.4 %shard_map.115 = (bf16[8,128,128]{2,1,0:T(8,128)(2,1)S(1)}, bf16[8,1,128,256]{3,2,1,0:T(8,128)(2,1)S(1)}, bf16[8,128,128]{2,1,0:T(8,128)(2,1)S(1)}, bf16[8,64,12...) custom-call(bf16[16,80,128]{2,1,0:T(8,128)(2,1)S(1)} %all-to-all-done.recv_ref, ...), custom_call_target="tpu_custom_call" | custom-call | tf_op jit(solution)/shard_map/pallas_call | solution.py:323
  23.0 0.0 collective-permute-done.other_ref
  23.0 1.1 %shard_map.116 = (bf16[16,64,128]{2,1,0:T(8,128)(2,1)S(1)}, bf16[8,64,128]{2,1,0:T(8,128)(2,1)S(1)}) custom-call(bf16[16,16,128]{2,1,0:T(8,128)(2,1)S(1)} %collective-permute-done.other_ref, f32[4,128,128]{2,1,0:T(8,128)S(1)} %get-tuple-element.38.term_ref, bf16[256,256]{1,0:T(8,128)(2,1)S(1)} %get-tuple-element.39.wo_ref, ...), custom_call_target="tpu_custom_call" | custom-call | tf_op jit(solution)/shard_map/pallas_call | solution.py:323
  24.1 13.3 %all_to_all.10.recv_ref = bf16[16,64,128]{2,1,0:T(8,128)(2,1)S(1)} all-to-all(bf16[16,64,128]{2,1,0:T(8,128)(2,1)S(1)} %get-tuple-element.52), channel_id=1, replica_groups=mesh['dp'=2,'head'=1,'row'=16] {'row'}, dimensions={0} | all-to-all | bytes 524288 | tf_op jit(solution)/shard_map/all_to_all | solution.py:339
  37.3 1.1 %shard_map.117 = (bf16[8,128,128]{2,1,0:T(8,128)(2,1)}, bf16[8,64,128]{2,1,0:T(8,128)(2,1)}) custom-call(bf16[16,64,128]{2,1,0:T(8,128)(2,1)S(1)} %all_to_all.10.recv_ref, bf16[8,64,128]{2,1,0:T(8,128)(2,1)S(1)} %get-tuple-element.53.mirror_ref, bf16[64,128]{1,0:T(8,128)(2,1)S(1)} %get-tuple-element.40.wd_ref, f32[64,128]{1,0:T(8,128)S(1)} %get-tuple-element.41.db_ref, ...), custom_call_target="tpu_custom_call" | custom-call | tf_op jit(solution)/shard_map/pallas_call | solution.py:323
  (3 shorter events, 0.0 us)
Async XLA Ops:
  2.8 7.6 %copy-start = (bf16[128,4,128]{2,1,0:T(4,128)(2,1)S(1)}, bf16[128,4,128]{2,1,0:T(4,128)(2,1)}, u32[]{:S(2)}) copy-start(bf16[128,4,128]{2,1,0:T(4,128)(2,1)} %w_ref.1) | copy-start | bytes 393220
  2.8 7.6 %copy-start.1 = (bf16[4,32,128]{2,1,0:T(8,128)(2,1)S(1)}, bf16[4,32,128]{2,1,0:T(8,128)(2,1)}, u32[]{:S(2)}) copy-start(bf16[4,32,128]{2,1,0:T(8,128)(2,1)} %param.17) | copy-start | bytes 98308
  2.8 7.6 %copy-start.2 = (bf16[128,64]{0,1:T(8,128)(2,1)S(1)}, bf16[128,64]{0,1:T(8,128)(2,1)}, u32[]{:S(2)}) copy-start(bf16[128,64]{0,1:T(8,128)(2,1)} %param.18) | copy-start | bytes 49156
  2.8 7.6 %copy-start.5 = (s32[128]{0:T(128)S(1)}, s32[128]{0:T(128)}, u32[]{:S(2)}) copy-start(s32[128]{0:T(128)} %param.11) | copy-start | bytes 1540
  2.8 7.6 %copy-start.6 = (s32[128]{0:T(128)S(1)}, s32[128]{0:T(128)}, u32[]{:S(2)}) copy-start(s32[128]{0:T(128)} %param.12) | copy-start | bytes 1540
  2.8 7.6 %copy-start.7 = (f32[64]{0:T(128)S(1)}, f32[64]{0:T(128)}, u32[]{:S(2)}) copy-start(f32[64]{0:T(128)} %param.19) | copy-start | bytes 772
  2.8 18.6 %all-to-all-start = ((bf16[16,80,128]{2,1,0:T(8,128)(2,1)}), bf16[16,80,128]{2,1,0:T(8,128)(2,1)S(1)}, u32[]{:S(2)}, u32[]{:S(2)}) async-start(bf16[16,80,128]{2,1,0:T(8,128)(2,1)} %shard_map.113), calls=%async_computation | async-start | bytes 655360 | tf_op jit(solution)/shard_map/all_to_all | solution.py:339
  10.4 0.7 %copy-start.3 = (f32[128]{0:T(128)S(1)}, f32[128]{0:T(128)}, u32[]{:S(2)}) copy-start(f32[128]{0:T(128)} %param.13) | copy-start | bytes 1540
  10.4 0.7 %copy-start.4 = (f32[2,4]{1,0:T(2,128)S(1)}, f32[2,4]{1,0:T(2,128)}, u32[]{:S(2)}) copy-start(f32[2,4]{1,0:T(2,128)} %cb_ref.1) | copy-start | bytes 100
  21.5 1.5 %collective-permute-start = (bf16[16,16,128]{2,1,0:T(8,128)(2,1)S(1)}, bf16[16,16,128]{2,1,0:T(8,128)(2,1)S(1)}, u32[]{:S(2)}, u32[]{:S(2)}) collective-permute-start(bf16[16,16,128]{2,1,0:T(8,128)(2,1)S(1)} %slice.3), channel_id=1, source_target_pairs={{0,1},{1,0},{2,3},{3,2},{4,5},{5,4},{6,7},{7,6},{8,9},{9,8},{10,11... | collective-permute-start | bytes 196616 | tf_op jit(solution)/shard_map/ppermute | solution.py:335
where the time goes:
time: 38.8 us; the launch traced here: 38.5 us
  blocking collectives  13.3 us (34%)
  waiting for transfers between devices  9.43 us (24%)
  starting transfers between devices  7.64 us (20%)
  Pallas kernels  6.68 us (17%)
  between operations  0.79 us (2%)
  local copies, waits for them, and re-layouts  0.66 us (2%)
    all_to_all x1, blocking collectives, all_to_all(): lax.all_to_all(blocks, 'row', split_axis=0, concat_axis=0, tiled=True)  13.3 us
    all_to_all x1, waiting for transfers between devices, all_to_all(): lax.all_to_all(blocks, 'row', split_axis=0, concat_axis=0, tiled=True)  9.43 us
    all_to_all x1, starting transfers between devices, all_to_all(): lax.all_to_all(blocks, 'row', split_axis=0, concat_axis=0, tiled=True)  7.53 us
    pallas_call x5, Pallas kernels, call(): pl.pallas_call(kernel, out_shape=[jax.ShapeDtypeStruct(s, d) for s, d in...  6.68 us
  transfers between devices with their start and end apart: 2, of which 1 were waited for; matrix products, arithmetic and copies ran while one was open for 0% of the time, Pallas kernels for 6%

commit v1 on v0

--- a/solution.py
+++ b/solution.py
@@ -32,16 +32,7 @@
     return (centered * lax.rsqrt(variance + 1e-05) * gain).astype(BF16)
 
 
-def swap_matrix(rows):
-    size = 2 * rows * rows
-    out = lax.broadcasted_iota(jnp.int32, (size, size), 0)
-    col = lax.broadcasted_iota(jnp.int32, (size, size), 1)
-    b, rest = out // (2 * rows), out % (2 * rows)
-    wanted = (rest // rows) * (rows * rows) + (rest % rows) * rows + b
-    return jnp.where(col == wanted, 1.0, 0.0).astype(BF16)
-
-
-def pack_kernel(x_hbm, gain_hbm, wb_hbm, out_hbm, x_ref, gain_ref, wb_ref, out_ref, sems, out_sems):
+def pack_kernel(x_hbm, gain_hbm, wb_hbm, out_hbm, x_ref, gain_ref, wb_ref, wide, out_ref, sems, out_sems):
     rows, n, chan = x_ref.shape
     peers = n // rows
     heads = wb_ref.shape[0]
@@ -71,9 +62,9 @@
     mine = [jnp.concatenate(mine[k : k + 2], 1) for k in range(0, rows, 2)]
     for copy in fetches:
         copy.wait()
-    for pair in range(rows // 2):
-        both = [x_ref[k].astype(F32).reshape(peers, rows, chan) for k in (2 * pair, 2 * pair + 1)]
-        out_ref[:, 2 * rows * pair : 2 * rows * (pair + 1), :] = jnp.concatenate(both, 1).astype(BF16)
+    for k in range(rows):
+        wide[:, pl.ds(k, rows, stride=rows), :] = x_ref[k].astype(F32).reshape(peers, rows, chan)
+    out_ref[:, :base, :] = wide[...].astype(BF16)
     store(0, base)
     normed = [layer_norm(x_ref[k].astype(F32), gain) for k in range(rows)]
     for pair in range(rows // 2):
@@ -90,12 +81,11 @@
 
 
 def prepare_kernel(
-    heads, rows,
+    heads,
     chain_ref, mask_ref, cb_ref, w_ref, db_ref, gain_ref, wo_ref, wd_ref,
-    term_ref, wt_ref, wk_out, dbc_ref, gain_out, wo_out, wd_out, swap_ref,
+    term_ref, wt_ref, wk_out, dbc_ref, gain_out, wo_out, wd_out,
 ):
     gain_out[...] = gain_ref[...]
-    swap_ref[...] = swap_matrix(rows)
     chan = w_ref.shape[0]
     width = wo_ref.shape[0]
     half = heads // 2
@@ -184,14 +174,14 @@
             body(i)
 
 
-def permuted(blocks, swap):
-    left, right = jnp.concatenate(blocks[:2], 0), jnp.concatenate(blocks[2:], 0)
-    return dot_nn(swap, jnp.concatenate([left, right], 1))
+def regrouped(left, right, rows):
+    both = [block.astype(F32).reshape(rows, rows, LANES) for block in (left, right)]
+    return jnp.concatenate(both, 1).reshape(2 * rows * rows, LANES)
 
 
 def project_kernel(
     heads,
-    recv_ref, gain_ref, w_ref, wk_ref, swap_ref, term_ref,
+    recv_ref, gain_ref, w_ref, wk_ref, term_ref,
     x_s, spread_s, k_s, v_s, g_s, gated_ref,
     n_s, own_spread, own_v, own_g, bias_s, inv_s, e_s,
 ):
@@ -202,18 +192,17 @@
     width = heads * dim
     base = rows * rows
     gain = gain_ref[...]
-    swap = swap_ref[...]
     group = 2 * rows
     w_k = wk_ref[...]
 
     quads = range(peers // 4)
-    x = [permuted([recv_ref[4 * quad + s, :base] for s in range(4)], swap) for quad in quads]
-    normed = [[layer_norm(two[:, :chan], gain), layer_norm(two[:, chan:], gain)] for two in x]
+    x = [[regrouped(recv_ref[s, :base], recv_ref[s + 1, :base], rows) for s in (4 * q, 4 * q + 2)] for q in quads]
+    normed = [[layer_norm(part, gain) for part in two] for two in x]
     keys = [dot_nt(jnp.concatenate(two, 1), w_k).astype(BF16) for two in normed]
     for quad in quads:
         for side in range(2):
             at = slice((2 * quad + side) * group, (2 * quad + side + 1) * group)
-            x_s[:, at, :] = x[quad][:, side * chan : (side + 1) * chan].astype(BF16).reshape(rows, group, chan)
+            x_s[:, at, :] = x[quad][side].astype(BF16).reshape(rows, group, chan)
             n_s[:, at, :] = normed[quad][side].reshape(rows, group, chan)
             k_s[:, at, :] = keys[quad][:, side * width : (side + 1) * width].reshape(rows, group, width)
 
@@ -250,7 +239,7 @@
     out_ref, *refs,
 ):
     if fused:
-        second_ref, bias_s, inv_s, e_s, gated_s, new_s = refs
+        second_ref, bias_s, inv_s, e_s, gated_s, new_s, wide = refs
     else:
         bias_s, inv_s, e_s, gated_s = refs
     peers = other_ref.shape[0]
@@ -279,12 +268,11 @@
 
     for j in range(0, rows, 2):
         update = updated(j // 2).astype(F32)
-        both = []
         for side in range(2):
             new = (x_s[j + side].astype(F32) + update[:, side * chan : (side + 1) * chan]).astype(BF16)
             new_s[j + side] = new
-            both.append(new.astype(F32).reshape(peers, rows, chan))
-        out_ref[:, j * rows : (j + 2) * rows, :] = jnp.concatenate(both, 1).astype(BF16)
+            wide[:, pl.ds(j + side, rows, stride=rows), :] = new.astype(F32).reshape(peers, rows, chan)
+    out_ref[...] = wide[...].astype(BF16)
     logits_of(new_s, wd_ref[...], db_ref[:, :1], second_ref)
 
 
@@ -295,16 +283,14 @@
         out_ref[j] = logits[:, j * n : (j + 1) * n].astype(BF16)
 
 
-def finish_kernel(recv_ref, mirror_ref, wd_ref, db_ref, swap_ref, new_hbm, dist_hbm, new_ref, dist_ref, sems):
+def finish_kernel(recv_ref, mirror_ref, wd_ref, db_ref, new_hbm, dist_hbm, new_ref, dist_ref, sems):
     peers, _, chan = recv_ref.shape
     rows = new_ref.shape[0]
     group = 2 * rows
-    swap = swap_ref[...]
-    for quad in range(peers // 4):
-        new = permuted([recv_ref[4 * quad + s] for s in range(4)], swap).astype(BF16)
-        for side in range(2):
-            at = slice((2 * quad + side) * group, (2 * quad + side + 1) * group)
-            new_ref[:, at, :] = new[:, side * chan : (side + 1) * chan].reshape(rows, group, chan)
+    for pair in range(peers // 2):
+        at = slice(pair * group, (pair + 1) * group)
+        block = regrouped(recv_ref[2 * pair], recv_ref[2 * pair + 1], rows)
+        new_ref[:, at, :] = block.astype(BF16).reshape(rows, group, chan)
     copies = [pltpu.make_async_copy(new_ref, new_hbm, sems.at[0])]
     copies[0].start()
     logits_of(new_ref, wd_ref[...], db_ref[:, :1], dist_ref)
@@ -361,6 +347,7 @@
             pltpu.VMEM(pair_act.shape, BF16),
             pltpu.VMEM(gain.shape, F32),
             pltpu.VMEM((heads, chan), BF16),
+            pltpu.VMEM((peers, base, chan), F32),
             pltpu.VMEM((peers, length, chan), BF16),
             pltpu.SemaphoreType.DMA((rows + 2,)),
             pltpu.SemaphoreType.DMA((2,)),
@@ -371,11 +358,10 @@
     )
     received = all_to_all(packed)
     prepared = call(
-        functools.partial(prepare_kernel, heads, rows),
+        functools.partial(prepare_kernel, heads),
         [
             ((heads, n, n), F32), ((3 * width, chan), BF16), ((2 * width, 2 * chan), BF16), ((bins, LANES), F32),
             ((1, chan), F32), ((2 * width, 2 * chan), BF16), ((bins, chan), BF16),
-            ((2 * base, 2 * base), BF16),
         ],
         [
             chain_id[None, :], residue_mask[None, :], chain_bias, w_proj, dist_bias[None, :],
@@ -384,7 +370,7 @@
         smem=(2,),
     )
     received, *prepared = lax.optimization_barrier((received, *prepared))
-    term, w_types, w_keys, db_col, gain, w_out, wd_t, swap = prepared
+    term, w_types, w_keys, db_col, gain, w_out, wd_t = prepared
     other_bias = swap_cores(received[:, base:])
     spread_shape = ((rows, tiles, width, heads // 2 * LANES), BF16)
     values_shape, gates_shape = ((rows, width // 2, n), BF16), ((rows, width // 2, n), F32)
@@ -403,7 +389,7 @@
             gates_shape,
             values_shape,
         ],
-        [received, gain, w_types, w_keys, swap, term],
+        [received, gain, w_types, w_keys, term],
         scratch=[
             pltpu.VMEM((rows, n, chan), BF16),
             *(pltpu.VMEM(*shape) for shape in (spread_shape, values_shape, gates_shape)),
@@ -418,7 +404,7 @@
         functools.partial(attend_kernel, fused),
         outs,
         [other_bias, term, w_out, wd_t, db_col, x_cols, spread, keys, values, gates, gated],
-        scratch=softmax_scratch + [pltpu.VMEM(*values_shape)] + [pltpu.VMEM((rows, n, chan), BF16)] * fused,
+        scratch=softmax_scratch + [pltpu.VMEM(*values_shape)] + [pltpu.VMEM((rows, n, chan), BF16), pltpu.VMEM((peers, base, chan), F32)] * fused,
     )
     if fused:
         to_rows, mirror = result
@@ -427,12 +413,12 @@
         new = (x_cols.astype(F32) + update).astype(BF16)
         logits = jnp.einsum("cb,jic->jbi", w_dist, new, preferred_element_type=F32)
         mirror = (logits + dist_bias[None, :, None]).astype(BF16)
-        to_rows = new.reshape(rows, peers, rows, chan).transpose(1, 0, 2, 3).reshape(peers, base, chan)
+        to_rows = new.reshape(rows, peers, rows, chan).transpose(1, 2, 0, 3).reshape(peers, base, chan)
     arrived = all_to_all(to_rows)
     new_rows, dist = call(
         finish_kernel,
         [((rows, n, chan), BF16), ((rows, bins, n), BF16)],
-        [arrived, mirror, wd_t, db_col, swap],
+        [arrived, mirror, wd_t, db_col],
         scratch=[
             pltpu.VMEM((rows, n, chan), BF16),
             pltpu.VMEM((rows, bins, n), BF16),

time: 38.8 us -> 38.6 us (level)
  no operation moved by 1% of the time
where the time goes in v1:
time: 38.6 us; the launch traced here: 38.3 us
  blocking collectives  13.2 us (34%)
  waiting for transfers between devices  9.46 us (25%)
  starting transfers between devices  7.64 us (20%)
  Pallas kernels  6.48 us (17%)
  between operations  0.78 us (2%)
  local copies, waits for them, and re-layouts  0.66 us (2%)
    all_to_all x1, blocking collectives, all_to_all(): lax.all_to_all(blocks, 'row', split_axis=0, concat_axis=0, tiled=True)  13.2 us
    all_to_all x1, waiting for transfers between devices, all_to_all(): lax.all_to_all(blocks, 'row', split_axis=0, concat_axis=0, tiled=True)  9.46 us
    all_to_all x1, starting transfers between devices, all_to_all(): lax.all_to_all(blocks, 'row', split_axis=0, concat_axis=0, tiled=True)  7.53 us
    pallas_call x5, Pallas kernels, call(): pl.pallas_call(kernel, out_shape=[jax.ShapeDtypeStruct(s, d) for s, d in...  6.48 us
  transfers between devices with their start and end apart: 2, of which 1 were waited for; matrix products, arithmetic and copies ran while one was open for 0% of the time, Pallas kernels for 6%

profile of v1, /device:TPU:0, one launch (start us, length us, event | category | flops | bytes accessed | tf_op | source)
XLA Modules:
  0.0 38.3 jit_solution(9078813399110752092)
XLA Ops:
  0.6 2.2 %shard_map.113 = bf16[16,80,128]{2,1,0:T(8,128)(2,1)} custom-call(bf16[8,128,128]{2,1,0:T(8,128)(2,1)} %x_hbm.1, f32[1,128]{1,0:T(1,128)} %bitcast.10, bf16[4,128]{1,0:T(4,128)(2,1)} %bitcast.15), custom_call_target="tpu_custom_call" | custom-call | tf_op jit(solution)/shard_map/pallas_call | solution.py:309
  2.9 0.0 copy-start
  2.9 0.0 copy-start.1
  2.9 0.0 copy-start.2
  2.9 0.0 copy-start.5
  2.9 0.0 copy-start.6
  2.9 0.0 copy-start.7
  2.9 7.5 %all-to-all-start = ((bf16[16,80,128]{2,1,0:T(8,128)(2,1)}), bf16[16,80,128]{2,1,0:T(8,128)(2,1)S(1)}, u32[]{:S(2)}, u32[]{:S(2)}) async-start(bf16[16,80,128]{2,1,0:T(8,128)(2,1)} %shard_map.113), calls=%async_computation | async-start | bytes 655360 | tf_op jit(solution)/shard_map/all_to_all | solution.py:325
  10.5 0.0 copy-start.3
  10.5 0.0 copy-start.4
  10.5 0.0 copy-done
  10.5 0.0 copy-done.1
  10.5 0.0 copy-done.2
  10.5 0.0 copy-done.5
  10.6 0.6 %copy-done.3 = f32[128]{0:T(128)S(1)} copy-done((f32[128]{0:T(128)S(1)}, f32[128]{0:T(128)}, u32[]{:S(2)}) %copy-start.3) | copy-done | bytes 536
  11.1 0.0 copy-done.4
  11.2 0.9 %shard_map.114 = (f32[4,128,128]{2,1,0:T(8,128)S(1)}, bf16[384,128]{1,0:T(8,128)(2,1)S(1)}, bf16[256,256]{1,0:T(8,128)(2,1)S(1)}, f32[64,128]{1,0:T(8,128)S(1)},...) custom-call(s32[1,128]{1,0:T(1,128)S(1)} %bitcast.12, s32[1,128]{1,0:T(1,128)S(1)} %bitcast.13, ...), custom_call_target="tpu_custom_call" | custom-call | tf_op jit(solution)/shard_map/pallas_call | solution.py:309
  12.1 9.5 %all-to-all-done.recv_ref = bf16[16,80,128]{2,1,0:T(8,128)(2,1)S(1)} async-done(((bf16[16,80,128]{2,1,0:T(8,128)(2,1)}), bf16[16,80,128]{2,1,0:T(8,128)(2,1)S(1)}, u32[]{:S(2)}, u32[]{:S(2)}) %all-to-all-start) | async-done | bytes 327712 | tf_op jit(solution)/shard_map/all_to_all | solution.py:325
  21.6 0.1 collective-permute-start
  21.7 1.2 %shard_map.115 = (bf16[8,128,128]{2,1,0:T(8,128)(2,1)S(1)}, bf16[8,1,128,256]{3,2,1,0:T(8,128)(2,1)S(1)}, bf16[8,128,128]{2,1,0:T(8,128)(2,1)S(1)}, bf16[8,64,12...) custom-call(bf16[16,80,128]{2,1,0:T(8,128)(2,1)S(1)} %all-to-all-done.recv_ref, ...), custom_call_target="tpu_custom_call" | custom-call | tf_op jit(solution)/shard_map/pallas_call | solution.py:309
  22.9 0.0 collective-permute-done.other_ref
  22.9 1.1 %shard_map.116 = (bf16[16,64,128]{2,1,0:T(8,128)(2,1)S(1)}, bf16[8,64,128]{2,1,0:T(8,128)(2,1)S(1)}) custom-call(bf16[16,16,128]{2,1,0:T(8,128)(2,1)S(1)} %collective-permute-done.other_ref, f32[4,128,128]{2,1,0:T(8,128)S(1)} %get-tuple-element.35.term_ref, bf16[256,256]{1,0:T(8,128)(2,1)S(1)} %get-tuple-element.36.wo_ref, ...), custom_call_target="tpu_custom_call" | custom-call | tf_op jit(solution)/shard_map/pallas_call | solution.py:309
  24.1 13.2 %all_to_all.10.recv_ref = bf16[16,64,128]{2,1,0:T(8,128)(2,1)S(1)} all-to-all(bf16[16,64,128]{2,1,0:T(8,128)(2,1)S(1)} %get-tuple-element.48), channel_id=1, replica_groups=mesh['dp'=2,'head'=1,'row'=16] {'row'}, dimensions={0} | all-to-all | bytes 524288 | tf_op jit(solution)/shard_map/all_to_all | solution.py:325
  37.3 0.9 %shard_map.117 = (bf16[8,128,128]{2,1,0:T(8,128)(2,1)}, bf16[8,64,128]{2,1,0:T(8,128)(2,1)}) custom-call(bf16[16,64,128]{2,1,0:T(8,128)(2,1)S(1)} %all_to_all.10.recv_ref, bf16[8,64,128]{2,1,0:T(8,128)(2,1)S(1)} %get-tuple-element.49.mirror_ref, bf16[64,128]{1,0:T(8,128)(2,1)S(1)} %get-tuple-element.37.wd_ref, f32[64,128]{1,0:T(8,128)S(1)} %get-tuple-element.38.db_ref), custom_call_target="tpu_custom_call" | custom-call | tf_op jit(solution)/shard_map/pallas_call | solution.py:309
  (3 shorter events, 0.0 us)
Async XLA Ops:
  2.9 7.6 %copy-start = (bf16[128,4,128]{2,1,0:T(4,128)(2,1)S(1)}, bf16[128,4,128]{2,1,0:T(4,128)(2,1)}, u32[]{:S(2)}) copy-start(bf16[128,4,128]{2,1,0:T(4,128)(2,1)} %w_ref.1) | copy-start | bytes 393220
  2.9 7.6 %copy-start.1 = (bf16[4,32,128]{2,1,0:T(8,128)(2,1)S(1)}, bf16[4,32,128]{2,1,0:T(8,128)(2,1)}, u32[]{:S(2)}) copy-start(bf16[4,32,128]{2,1,0:T(8,128)(2,1)} %param.17) | copy-start | bytes 98308
  2.9 7.6 %copy-start.2 = (bf16[128,64]{0,1:T(8,128)(2,1)S(1)}, bf16[128,64]{0,1:T(8,128)(2,1)}, u32[]{:S(2)}) copy-start(bf16[128,64]{0,1:T(8,128)(2,1)} %param.18) | copy-start | bytes 49156
  2.9 7.6 %copy-start.5 = (s32[128]{0:T(128)S(1)}, s32[128]{0:T(128)}, u32[]{:S(2)}) copy-start(s32[128]{0:T(128)} %param.11) | copy-start | bytes 1540
  2.9 7.6 %copy-start.6 = (s32[128]{0:T(128)S(1)}, s32[128]{0:T(128)}, u32[]{:S(2)}) copy-start(s32[128]{0:T(128)} %param.12) | copy-start | bytes 1540
  2.9 7.6 %copy-start.7 = (f32[64]{0:T(128)S(1)}, f32[64]{0:T(128)}, u32[]{:S(2)}) copy-start(f32[64]{0:T(128)} %param.19) | copy-start | bytes 772
  2.9 18.6 %all-to-all-start = ((bf16[16,80,128]{2,1,0:T(8,128)(2,1)}), bf16[16,80,128]{2,1,0:T(8,128)(2,1)S(1)}, u32[]{:S(2)}, u32[]{:S(2)}) async-start(bf16[16,80,128]{2,1,0:T(8,128)(2,1)} %shard_map.113), calls=%async_computation | async-start | bytes 655360 | tf_op jit(solution)/shard_map/all_to_all | solution.py:325
  10.5 0.7 %copy-start.3 = (f32[128]{0:T(128)S(1)}, f32[128]{0:T(128)}, u32[]{:S(2)}) copy-start(f32[128]{0:T(128)} %param.13) | copy-start | bytes 1540
  10.5 0.7 %copy-start.4 = (f32[2,4]{1,0:T(2,128)S(1)}, f32[2,4]{1,0:T(2,128)}, u32[]{:S(2)}) copy-start(f32[2,4]{1,0:T(2,128)} %cb_ref.1) | copy-start | bytes 100
  21.6 1.4 %collective-permute-start = (bf16[16,16,128]{2,1,0:T(8,128)(2,1)S(1)}, bf16[16,16,128]{2,1,0:T(8,128)(2,1)S(1)}, u32[]{:S(2)}, u32[]{:S(2)}) collective-permute-start(bf16[16,16,128]{2,1,0:T(8,128)(2,1)S(1)} %slice.3), channel_id=1, source_target_pairs={{0,1},{1,0},{2,3},{3,2},{4,5},{5,4},{6,7},{7,6},{8,9},{9,8},{10,11... | collective-permute-start | bytes 196616 | tf_op jit(solution)/shard_map/ppermute | solution.py:321

commit v2 on v1

--- a/solution.py
+++ b/solution.py
@@ -62,11 +62,11 @@
     mine = [jnp.concatenate(mine[k : k + 2], 1) for k in range(0, rows, 2)]
     for copy in fetches:
         copy.wait()
+    normed = [layer_norm(x_ref[k].astype(F32), gain) for k in range(rows)]
     for k in range(rows):
         wide[:, pl.ds(k, rows, stride=rows), :] = x_ref[k].astype(F32).reshape(peers, rows, chan)
     out_ref[:, :base, :] = wide[...].astype(BF16)
     store(0, base)
-    normed = [layer_norm(x_ref[k].astype(F32), gain) for k in range(rows)]
     for pair in range(rows // 2):
         bias = bias + dot_nt(mine[pair], jnp.concatenate(normed[2 * pair : 2 * pair + 2], 1))
     bias = bias.astype(BF16)
@@ -287,18 +287,22 @@
     peers, _, chan = recv_ref.shape
     rows = new_ref.shape[0]
     group = 2 * rows
+    share = peers // 4
+    copies = []
     for pair in range(peers // 2):
         at = slice(pair * group, (pair + 1) * group)
         block = regrouped(recv_ref[2 * pair], recv_ref[2 * pair + 1], rows)
         new_ref[:, at, :] = block.astype(BF16).reshape(rows, group, chan)
-    copies = [pltpu.make_async_copy(new_ref, new_hbm, sems.at[0])]
-    copies[0].start()
+        if (pair + 1) % share == 0:
+            at = pl.ds((pair + 1 - share) * group, share * group)
+            copies.append(pltpu.make_async_copy(new_ref.at[:, at, :], new_hbm.at[:, at, :], sems.at[len(copies)]))
+            copies[-1].start()
     logits_of(new_ref, wd_ref[...], db_ref[:, :1], dist_ref)
     for i in range(rows):
         dist_ref[i] = (dist_ref[i].astype(F32) + mirror_ref[i].astype(F32)).astype(BF16)
         if i % 2:
             at = pl.ds(i - 1, 2)
-            copies.append(pltpu.make_async_copy(dist_ref.at[at], dist_hbm.at[at], sems.at[1 + i // 2]))
+            copies.append(pltpu.make_async_copy(dist_ref.at[at], dist_hbm.at[at], sems.at[len(copies)]))
             copies[-1].start()
     for copy in copies:
         copy.wait()
@@ -422,7 +426,7 @@
         scratch=[
             pltpu.VMEM((rows, n, chan), BF16),
             pltpu.VMEM((rows, bins, n), BF16),
-            pltpu.SemaphoreType.DMA((1 + rows // 2,)),
+            pltpu.SemaphoreType.DMA((2 + rows // 2,)),
         ],
         hbm_outs=True,
     )

time: 38.6 us -> 38.6 us (level)
  no operation moved by 1% of the time
where the time goes in v2:
time: 38.6 us; the launch traced here: 38.2 us
  blocking collectives  13.2 us (34%)
  waiting for transfers between devices  9.46 us (25%)
  starting transfers between devices  7.64 us (20%)
  Pallas kernels  6.42 us (17%)
  between operations  0.78 us (2%)
  local copies, waits for them, and re-layouts  0.66 us (2%)
    all_to_all x1, blocking collectives, all_to_all(): lax.all_to_all(blocks, 'row', split_axis=0, concat_axis=0, tiled=True)  13.2 us
    all_to_all x1, waiting for transfers between devices, all_to_all(): lax.all_to_all(blocks, 'row', split_axis=0, concat_axis=0, tiled=True)  9.46 us
    all_to_all x1, starting transfers between devices, all_to_all(): lax.all_to_all(blocks, 'row', split_axis=0, concat_axis=0, tiled=True)  7.53 us
    pallas_call x5, Pallas kernels, call(): pl.pallas_call(kernel, out_shape=[jax.ShapeDtypeStruct(s, d) for s, d in...  6.42 us
  transfers between devices with their start and end apart: 2, of which 1 were waited for; matrix products, arithmetic and copies ran while one was open for 0% of the time, Pallas kernels for 6%

profile of v2, /device:TPU:0, one launch (start us, length us, event | category | flops | bytes accessed | tf_op | source)
XLA Modules:
  0.0 38.2 jit_solution(5971858968319037375)
XLA Ops:
  0.6 2.2 %shard_map.113 = bf16[16,80,128]{2,1,0:T(8,128)(2,1)} custom-call(bf16[8,128,128]{2,1,0:T(8,128)(2,1)} %x_hbm.1, f32[1,128]{1,0:T(1,128)} %bitcast.10, bf16[4,128]{1,0:T(4,128)(2,1)} %bitcast.15), custom_call_target="tpu_custom_call" | custom-call | tf_op jit(solution)/shard_map/pallas_call | solution.py:313
  2.8 0.0 copy-start
  2.8 0.0 copy-start.1
  2.8 0.0 copy-start.2
  2.8 0.0 copy-start.5
  2.8 0.0 copy-start.6
  2.9 0.0 copy-start.7
  2.9 7.5 %all-to-all-start = ((bf16[16,80,128]{2,1,0:T(8,128)(2,1)}), bf16[16,80,128]{2,1,0:T(8,128)(2,1)S(1)}, u32[]{:S(2)}, u32[]{:S(2)}) async-start(bf16[16,80,128]{2,1,0:T(8,128)(2,1)} %shard_map.113), calls=%async_computation | async-start | bytes 655360 | tf_op jit(solution)/shard_map/all_to_all | solution.py:329
  10.4 0.0 copy-start.3
  10.4 0.0 copy-start.4
  10.4 0.0 copy-done
  10.4 0.0 copy-done.1
  10.5 0.0 copy-done.2
  10.5 0.0 copy-done.5
  10.5 0.6 %copy-done.3 = f32[128]{0:T(128)S(1)} copy-done((f32[128]{0:T(128)S(1)}, f32[128]{0:T(128)}, u32[]{:S(2)}) %copy-start.3) | copy-done | bytes 536
  11.1 0.0 copy-done.4
  11.1 0.9 %shard_map.114 = (f32[4,128,128]{2,1,0:T(8,128)S(1)}, bf16[384,128]{1,0:T(8,128)(2,1)S(1)}, bf16[256,256]{1,0:T(8,128)(2,1)S(1)}, f32[64,128]{1,0:T(8,128)S(1)},...) custom-call(s32[1,128]{1,0:T(1,128)S(1)} %bitcast.12, s32[1,128]{1,0:T(1,128)S(1)} %bitcast.13, ...), custom_call_target="tpu_custom_call" | custom-call | tf_op jit(solution)/shard_map/pallas_call | solution.py:313
  12.0 9.5 %all-to-all-done.recv_ref = bf16[16,80,128]{2,1,0:T(8,128)(2,1)S(1)} async-done(((bf16[16,80,128]{2,1,0:T(8,128)(2,1)}), bf16[16,80,128]{2,1,0:T(8,128)(2,1)S(1)}, u32[]{:S(2)}, u32[]{:S(2)}) %all-to-all-start) | async-done | bytes 327712 | tf_op jit(solution)/shard_map/all_to_all | solution.py:329
  21.5 0.1 collective-permute-start
  21.6 1.2 %shard_map.115 = (bf16[8,128,128]{2,1,0:T(8,128)(2,1)S(1)}, bf16[8,1,128,256]{3,2,1,0:T(8,128)(2,1)S(1)}, bf16[8,128,128]{2,1,0:T(8,128)(2,1)S(1)}, bf16[8,64,12...) custom-call(bf16[16,80,128]{2,1,0:T(8,128)(2,1)S(1)} %all-to-all-done.recv_ref, ...), custom_call_target="tpu_custom_call" | custom-call | tf_op jit(solution)/shard_map/pallas_call | solution.py:313
  22.9 0.0 collective-permute-done.other_ref
  22.9 1.1 %shard_map.116 = (bf16[16,64,128]{2,1,0:T(8,128)(2,1)S(1)}, bf16[8,64,128]{2,1,0:T(8,128)(2,1)S(1)}) custom-call(bf16[16,16,128]{2,1,0:T(8,128)(2,1)S(1)} %collective-permute-done.other_ref, f32[4,128,128]{2,1,0:T(8,128)S(1)} %get-tuple-element.35.term_ref, bf16[256,256]{1,0:T(8,128)(2,1)S(1)} %get-tuple-element.36.wo_ref, ...), custom_call_target="tpu_custom_call" | custom-call | tf_op jit(solution)/shard_map/pallas_call | solution.py:313
  24.0 13.2 %all_to_all.10.recv_ref = bf16[16,64,128]{2,1,0:T(8,128)(2,1)S(1)} all-to-all(bf16[16,64,128]{2,1,0:T(8,128)(2,1)S(1)} %get-tuple-element.48), channel_id=1, replica_groups=mesh['dp'=2,'head'=1,'row'=16] {'row'}, dimensions={0} | all-to-all | bytes 524288 | tf_op jit(solution)/shard_map/all_to_all | solution.py:329
  37.3 1.0 %shard_map.117 = (bf16[8,128,128]{2,1,0:T(8,128)(2,1)}, bf16[8,64,128]{2,1,0:T(8,128)(2,1)}) custom-call(bf16[16,64,128]{2,1,0:T(8,128)(2,1)S(1)} %all_to_all.10.recv_ref, bf16[8,64,128]{2,1,0:T(8,128)(2,1)S(1)} %get-tuple-element.49.mirror_ref, bf16[64,128]{1,0:T(8,128)(2,1)S(1)} %get-tuple-element.37.wd_ref, f32[64,128]{1,0:T(8,128)S(1)} %get-tuple-element.38.db_ref), custom_call_target="tpu_custom_call" | custom-call | tf_op jit(solution)/shard_map/pallas_call | solution.py:313
  (3 shorter events, 0.0 us)
Async XLA Ops:
  2.8 7.6 %copy-start = (bf16[128,4,128]{2,1,0:T(4,128)(2,1)S(1)}, bf16[128,4,128]{2,1,0:T(4,128)(2,1)}, u32[]{:S(2)}) copy-start(bf16[128,4,128]{2,1,0:T(4,128)(2,1)} %w_ref.1) | copy-start | bytes 393220
  2.8 7.6 %copy-start.1 = (bf16[4,32,128]{2,1,0:T(8,128)(2,1)S(1)}, bf16[4,32,128]{2,1,0:T(8,128)(2,1)}, u32[]{:S(2)}) copy-start(bf16[4,32,128]{2,1,0:T(8,128)(2,1)} %param.17) | copy-start | bytes 98308
  2.8 7.6 %copy-start.2 = (bf16[128,64]{0,1:T(8,128)(2,1)S(1)}, bf16[128,64]{0,1:T(8,128)(2,1)}, u32[]{:S(2)}) copy-start(bf16[128,64]{0,1:T(8,128)(2,1)} %param.18) | copy-start | bytes 49156
  2.8 7.6 %copy-start.5 = (s32[128]{0:T(128)S(1)}, s32[128]{0:T(128)}, u32[]{:S(2)}) copy-start(s32[128]{0:T(128)} %param.11) | copy-start | bytes 1540
  2.8 7.6 %copy-start.6 = (s32[128]{0:T(128)S(1)}, s32[128]{0:T(128)}, u32[]{:S(2)}) copy-start(s32[128]{0:T(128)} %param.12) | copy-start | bytes 1540
  2.9 7.6 %copy-start.7 = (f32[64]{0:T(128)S(1)}, f32[64]{0:T(128)}, u32[]{:S(2)}) copy-start(f32[64]{0:T(128)} %param.19) | copy-start | bytes 772
  2.9 18.6 %all-to-all-start = ((bf16[16,80,128]{2,1,0:T(8,128)(2,1)}), bf16[16,80,128]{2,1,0:T(8,128)(2,1)S(1)}, u32[]{:S(2)}, u32[]{:S(2)}) async-start(bf16[16,80,128]{2,1,0:T(8,128)(2,1)} %shard_map.113), calls=%async_computation | async-start | bytes 655360 | tf_op jit(solution)/shard_map/all_to_all | solution.py:329
  10.4 0.7 %copy-start.3 = (f32[128]{0:T(128)S(1)}, f32[128]{0:T(128)}, u32[]{:S(2)}) copy-start(f32[128]{0:T(128)} %param.13) | copy-start | bytes 1540
  10.4 0.7 %copy-start.4 = (f32[2,4]{1,0:T(2,128)S(1)}, f32[2,4]{1,0:T(2,128)}, u32[]{:S(2)}) copy-start(f32[2,4]{1,0:T(2,128)} %cb_ref.1) | copy-start | bytes 100
  21.5 1.4 %collective-permute-start = (bf16[16,16,128]{2,1,0:T(8,128)(2,1)S(1)}, bf16[16,16,128]{2,1,0:T(8,128)(2,1)S(1)}, u32[]{:S(2)}, u32[]{:S(2)}) collective-permute-start(bf16[16,16,128]{2,1,0:T(8,128)(2,1)S(1)} %slice.3), channel_id=1, source_target_pairs={{0,1},{1,0},{2,3},{3,2},{4,5},{5,4},{6,7},{7,6},{8,9},{9,8},{10,11... | collective-permute-start | bytes 196616 | tf_op jit(solution)/shard_map/ppermute | solution.py:325

commit v3 on v2

--- a/solution.py
+++ b/solution.py
@@ -38,10 +38,11 @@
     heads = wb_ref.shape[0]
     half = heads * rows // 2
     base = rows * rows
-    fetch_gain = pltpu.make_async_copy(gain_hbm, gain_ref, sems.at[rows])
-    fetch_wb = pltpu.make_async_copy(wb_hbm, wb_ref, sems.at[rows + 1])
-    fetches = [pltpu.make_async_copy(x_hbm.at[k], x_ref.at[k], sems.at[k]) for k in range(rows)]
-    for copy in (fetch_gain, fetch_wb, *fetches):
+    fetch_gain = pltpu.make_async_copy(gain_hbm, gain_ref, sems.at[2])
+    fetch_wb = pltpu.make_async_copy(wb_hbm, wb_ref, sems.at[3])
+    parts = [pl.ds(part * rows // 2, rows // 2) for part in range(2)]
+    fetches = [pltpu.make_async_copy(x_hbm.at[at], x_ref.at[at], sems.at[i]) for i, at in enumerate(parts)]
+    for copy in (*fetches, fetch_gain, fetch_wb):
         copy.start()
     stores = []
 
@@ -353,7 +354,7 @@
             pltpu.VMEM((heads, chan), BF16),
             pltpu.VMEM((peers, base, chan), F32),
             pltpu.VMEM((peers, length, chan), BF16),
-            pltpu.SemaphoreType.DMA((rows + 2,)),
+            pltpu.SemaphoreType.DMA((4,)),
             pltpu.SemaphoreType.DMA((2,)),
         ],
         hbm=(0, 1, 2),

time: 38.6 us -> 38.5 us (level)
  no operation moved by 1% of the time
where the time goes in v3:
time: 38.5 us; the launch traced here: 38.2 us
  blocking collectives  13.2 us (34%)
  waiting for transfers between devices  9.46 us (25%)
  starting transfers between devices  7.64 us (20%)
  Pallas kernels  6.43 us (17%)
  between operations  0.78 us (2%)
  local copies, waits for them, and re-layouts  0.66 us (2%)
    all_to_all x1, blocking collectives, all_to_all(): lax.all_to_all(blocks, 'row', split_axis=0, concat_axis=0, tiled=True)  13.2 us
    all_to_all x1, waiting for transfers between devices, all_to_all(): lax.all_to_all(blocks, 'row', split_axis=0, concat_axis=0, tiled=True)  9.46 us
    all_to_all x1, starting transfers between devices, all_to_all(): lax.all_to_all(blocks, 'row', split_axis=0, concat_axis=0, tiled=True)  7.53 us
    pallas_call x5, Pallas kernels, call(): pl.pallas_call(kernel, out_shape=[jax.ShapeDtypeStruct(s, d) for s, d in...  6.43 us
  transfers between devices with their start and end apart: 2, of which 1 were waited for; matrix products, arithmetic and copies ran while one was open for 0% of the time, Pallas kernels for 6%

profile of v3, /device:TPU:0, one launch (start us, length us, event | category | flops | bytes accessed | tf_op | source)
XLA Modules:
  0.0 38.2 jit_solution(7067318513801307874)
XLA Ops:
  0.6 2.2 %shard_map.113 = bf16[16,80,128]{2,1,0:T(8,128)(2,1)} custom-call(bf16[8,128,128]{2,1,0:T(8,128)(2,1)} %x_hbm.1, f32[1,128]{1,0:T(1,128)} %bitcast.10, bf16[4,128]{1,0:T(4,128)(2,1)} %bitcast.15), custom_call_target="tpu_custom_call" | custom-call | tf_op jit(solution)/shard_map/pallas_call | solution.py:314
  2.8 0.0 copy-start
  2.8 0.0 copy-start.1
  2.8 0.0 copy-start.2
  2.8 0.0 copy-start.5
  2.9 0.0 copy-start.6
  2.9 0.0 copy-start.7
  2.9 7.5 %all-to-all-start = ((bf16[16,80,128]{2,1,0:T(8,128)(2,1)}), bf16[16,80,128]{2,1,0:T(8,128)(2,1)S(1)}, u32[]{:S(2)}, u32[]{:S(2)}) async-start(bf16[16,80,128]{2,1,0:T(8,128)(2,1)} %shard_map.113), calls=%async_computation | async-start | bytes 655360 | tf_op jit(solution)/shard_map/all_to_all | solution.py:330
  10.4 0.0 copy-start.3
  10.4 0.0 copy-start.4
  10.4 0.0 copy-done
  10.5 0.0 copy-done.1
  10.5 0.0 copy-done.2
  10.5 0.0 copy-done.5
  10.5 0.6 %copy-done.3 = f32[128]{0:T(128)S(1)} copy-done((f32[128]{0:T(128)S(1)}, f32[128]{0:T(128)}, u32[]{:S(2)}) %copy-start.3) | copy-done | bytes 536
  11.1 0.0 copy-done.4
  11.1 0.9 %shard_map.114 = (f32[4,128,128]{2,1,0:T(8,128)S(1)}, bf16[384,128]{1,0:T(8,128)(2,1)S(1)}, bf16[256,256]{1,0:T(8,128)(2,1)S(1)}, f32[64,128]{1,0:T(8,128)S(1)},...) custom-call(s32[1,128]{1,0:T(1,128)S(1)} %bitcast.12, s32[1,128]{1,0:T(1,128)S(1)} %bitcast.13, ...), custom_call_target="tpu_custom_call" | custom-call | tf_op jit(solution)/shard_map/pallas_call | solution.py:314
  12.1 9.5 %all-to-all-done.recv_ref = bf16[16,80,128]{2,1,0:T(8,128)(2,1)S(1)} async-done(((bf16[16,80,128]{2,1,0:T(8,128)(2,1)}), bf16[16,80,128]{2,1,0:T(8,128)(2,1)S(1)}, u32[]{:S(2)}, u32[]{:S(2)}) %all-to-all-start) | async-done | bytes 327712 | tf_op jit(solution)/shard_map/all_to_all | solution.py:330
  21.5 0.1 collective-permute-start
  21.6 1.2 %shard_map.115 = (bf16[8,128,128]{2,1,0:T(8,128)(2,1)S(1)}, bf16[8,1,128,256]{3,2,1,0:T(8,128)(2,1)S(1)}, bf16[8,128,128]{2,1,0:T(8,128)(2,1)S(1)}, bf16[8,64,12...) custom-call(bf16[16,80,128]{2,1,0:T(8,128)(2,1)S(1)} %all-to-all-done.recv_ref, ...), custom_call_target="tpu_custom_call" | custom-call | tf_op jit(solution)/shard_map/pallas_call | solution.py:314
  22.9 0.0 collective-permute-done.other_ref
  22.9 1.1 %shard_map.116 = (bf16[16,64,128]{2,1,0:T(8,128)(2,1)S(1)}, bf16[8,64,128]{2,1,0:T(8,128)(2,1)S(1)}) custom-call(bf16[16,16,128]{2,1,0:T(8,128)(2,1)S(1)} %collective-permute-done.other_ref, f32[4,128,128]{2,1,0:T(8,128)S(1)} %get-tuple-element.35.term_ref, bf16[256,256]{1,0:T(8,128)(2,1)S(1)} %get-tuple-element.36.wo_ref, ...), custom_call_target="tpu_custom_call" | custom-call | tf_op jit(solution)/shard_map/pallas_call | solution.py:314
  24.0 13.2 %all_to_all.10.recv_ref = bf16[16,64,128]{2,1,0:T(8,128)(2,1)S(1)} all-to-all(bf16[16,64,128]{2,1,0:T(8,128)(2,1)S(1)} %get-tuple-element.48), channel_id=1, replica_groups=mesh['dp'=2,'head'=1,'row'=16] {'row'}, dimensions={0} | all-to-all | bytes 524288 | tf_op jit(solution)/shard_map/all_to_all | solution.py:330
  37.3 1.0 %shard_map.117 = (bf16[8,128,128]{2,1,0:T(8,128)(2,1)}, bf16[8,64,128]{2,1,0:T(8,128)(2,1)}) custom-call(bf16[16,64,128]{2,1,0:T(8,128)(2,1)S(1)} %all_to_all.10.recv_ref, bf16[8,64,128]{2,1,0:T(8,128)(2,1)S(1)} %get-tuple-element.49.mirror_ref, bf16[64,128]{1,0:T(8,128)(2,1)S(1)} %get-tuple-element.37.wd_ref, f32[64,128]{1,0:T(8,128)S(1)} %get-tuple-element.38.db_ref), custom_call_target="tpu_custom_call" | custom-call | tf_op jit(solution)/shard_map/pallas_call | solution.py:314
  (3 shorter events, 0.0 us)
Async XLA Ops:
  2.8 7.6 %copy-start = (bf16[128,4,128]{2,1,0:T(4,128)(2,1)S(1)}, bf16[128,4,128]{2,1,0:T(4,128)(2,1)}, u32[]{:S(2)}) copy-start(bf16[128,4,128]{2,1,0:T(4,128)(2,1)} %w_ref.1) | copy-start | bytes 393220
  2.8 7.6 %copy-start.1 = (bf16[4,32,128]{2,1,0:T(8,128)(2,1)S(1)}, bf16[4,32,128]{2,1,0:T(8,128)(2,1)}, u32[]{:S(2)}) copy-start(bf16[4,32,128]{2,1,0:T(8,128)(2,1)} %param.17) | copy-start | bytes 98308
  2.8 7.6 %copy-start.2 = (bf16[128,64]{0,1:T(8,128)(2,1)S(1)}, bf16[128,64]{0,1:T(8,128)(2,1)}, u32[]{:S(2)}) copy-start(bf16[128,64]{0,1:T(8,128)(2,1)} %param.18) | copy-start | bytes 49156
  2.8 7.6 %copy-start.5 = (s32[128]{0:T(128)S(1)}, s32[128]{0:T(128)}, u32[]{:S(2)}) copy-start(s32[128]{0:T(128)} %param.11) | copy-start | bytes 1540
  2.9 7.6 %copy-start.6 = (s32[128]{0:T(128)S(1)}, s32[128]{0:T(128)}, u32[]{:S(2)}) copy-start(s32[128]{0:T(128)} %param.12) | copy-start | bytes 1540
  2.9 7.6 %copy-start.7 = (f32[64]{0:T(128)S(1)}, f32[64]{0:T(128)}, u32[]{:S(2)}) copy-start(f32[64]{0:T(128)} %param.19) | copy-start | bytes 772
  2.9 18.6 %all-to-all-start = ((bf16[16,80,128]{2,1,0:T(8,128)(2,1)}), bf16[16,80,128]{2,1,0:T(8,128)(2,1)S(1)}, u32[]{:S(2)}, u32[]{:S(2)}) async-start(bf16[16,80,128]{2,1,0:T(8,128)(2,1)} %shard_map.113), calls=%async_computation | async-start | bytes 655360 | tf_op jit(solution)/shard_map/all_to_all | solution.py:330
  10.4 0.7 %copy-start.3 = (f32[128]{0:T(128)S(1)}, f32[128]{0:T(128)}, u32[]{:S(2)}) copy-start(f32[128]{0:T(128)} %param.13) | copy-start | bytes 1540
  10.4 0.7 %copy-start.4 = (f32[2,4]{1,0:T(2,128)S(1)}, f32[2,4]{1,0:T(2,128)}, u32[]{:S(2)}) copy-start(f32[2,4]{1,0:T(2,128)} %cb_ref.1) | copy-start | bytes 100
  21.5 1.4 %collective-permute-start = (bf16[16,16,128]{2,1,0:T(8,128)(2,1)S(1)}, bf16[16,16,128]{2,1,0:T(8,128)(2,1)S(1)}, u32[]{:S(2)}, u32[]{:S(2)}) collective-permute-start(bf16[16,16,128]{2,1,0:T(8,128)(2,1)S(1)} %slice.3), channel_id=1, source_target_pairs={{0,1},{1,0},{2,3},{3,2},{4,5},{5,4},{6,7},{7,6},{8,9},{9,8},{10,11... | collective-permute-start | bytes 196616 | tf_op jit(solution)/shard_map/ppermute | solution.py:326

commit v4 on v2

--- a/solution.py
+++ b/solution.py
@@ -235,11 +235,11 @@
 
 def attend_kernel(
     fused,
-    other_ref, term_ref, wo_ref, wd_ref, db_ref, x_s, spread_s, k_s, v_s, g_s, gated_ref,
+    other_ref, term_ref, wo_ref, x_s, spread_s, k_s, v_s, g_s, gated_ref,
     out_ref, *refs,
 ):
     if fused:
-        second_ref, bias_s, inv_s, e_s, gated_s, new_s, wide = refs
+        new_s, bias_s, inv_s, e_s, gated_s, wide = refs
     else:
         bias_s, inv_s, e_s, gated_s = refs
     peers = other_ref.shape[0]
@@ -273,7 +273,10 @@
             new_s[j + side] = new
             wide[:, pl.ds(j + side, rows, stride=rows), :] = new.astype(F32).reshape(peers, rows, chan)
     out_ref[...] = wide[...].astype(BF16)
-    logits_of(new_s, wd_ref[...], db_ref[:, :1], second_ref)
+
+
+def mirror_kernel(new_ref, wd_ref, db_ref, out_ref):
+    logits_of(new_ref, wd_ref[...], db_ref[:, :1], out_ref)
 
 
 def logits_of(new_ref, w_dist, d_bias, out_ref):
@@ -401,24 +404,24 @@
         ],
     )
     if fused:
-        outs = [((peers, base, chan), BF16), ((rows, bins, n), BF16)]
+        outs = [((peers, base, chan), BF16), ((rows, n, chan), BF16)]
     else:
         outs = [((rows, n, chan), BF16)]
     result = call(
         functools.partial(attend_kernel, fused),
         outs,
-        [other_bias, term, w_out, wd_t, db_col, x_cols, spread, keys, values, gates, gated],
-        scratch=softmax_scratch + [pltpu.VMEM(*values_shape)] + [pltpu.VMEM((rows, n, chan), BF16), pltpu.VMEM((peers, base, chan), F32)] * fused,
+        [other_bias, term, w_out, x_cols, spread, keys, values, gates, gated],
+        scratch=softmax_scratch + [pltpu.VMEM(*values_shape)] + [pltpu.VMEM((peers, base, chan), F32)] * fused,
     )
     if fused:
-        to_rows, mirror = result
+        to_rows, new = result
     else:
         update = lax.psum(result[0], "head").astype(F32)
         new = (x_cols.astype(F32) + update).astype(BF16)
-        logits = jnp.einsum("cb,jic->jbi", w_dist, new, preferred_element_type=F32)
-        mirror = (logits + dist_bias[None, :, None]).astype(BF16)
         to_rows = new.reshape(rows, peers, rows, chan).transpose(1, 2, 0, 3).reshape(peers, base, chan)
     arrived = all_to_all(to_rows)
+    (mirror,) = call(mirror_kernel, [((rows, bins, n), BF16)], [new, wd_t, db_col])
+    arrived, mirror = lax.optimization_barrier((arrived, mirror))
     new_rows, dist = call(
         finish_kernel,
         [((rows, n, chan), BF16), ((rows, bins, n), BF16)],

time: 38.6 us -> 39.5 us (1.023)
  blocking collectives: 13.2 us -> 0 us
  waiting for transfers between devices: 9.46 us -> 19.3 us
  starting transfers between devices: 7.64 us -> 11.2 us
  Pallas kernels: 6.42 us -> 7.19 us
    all_to_all x1 -> x0, blocking collectives: 13.2 us -> none  [all_to_all(): lax.all_to_all(blocks, 'row', split_axis=0, concat_axis=0, tiled=True)]
    all_to_all x1 -> x2, waiting for transfers between devices: 9.46 us -> 19.2 us  [all_to_all(): lax.all_to_all(blocks, 'row', split_axis=0, concat_axis=0, tiled=True)]
    all_to_all x1 -> x2, starting transfers between devices: 7.53 us -> 11.1 us  [all_to_all(): lax.all_to_all(blocks, 'row', split_axis=0, concat_axis=0, tiled=True)]
    pallas_call x5 -> x6, Pallas kernels: 6.42 us -> 7.19 us  [call(): pl.pallas_call(kernel, out_shape=[jax.ShapeDtypeStruct(s, d) for s, d in...]
  transfers between devices with their start and end apart: 2 -> 3, of which waited for: 1 -> 2; matrix products, arithmetic and copies ran while one was open for 0% -> 0% of each run, Pallas kernels for 6% -> 6%
where the time goes in v4:
time: 39.5 us; the launch traced here: 39.1 us
  waiting for transfers between devices  19.3 us (49%)
  starting transfers between devices  11.2 us (28%)
  Pallas kernels  7.19 us (18%)
  between operations  0.79 us (2%)
  local copies, waits for them, and re-layouts  0.66 us (2%)
    all_to_all x2, waiting for transfers between devices, all_to_all(): lax.all_to_all(blocks, 'row', split_axis=0, concat_axis=0, tiled=True)  19.2 us
    all_to_all x2, starting transfers between devices, all_to_all(): lax.all_to_all(blocks, 'row', split_axis=0, concat_axis=0, tiled=True)  11.1 us
    pallas_call x6, Pallas kernels, call(): pl.pallas_call(kernel, out_shape=[jax.ShapeDtypeStruct(s, d) for s, d in...  7.19 us
  transfers between devices with their start and end apart: 3, of which 2 were waited for; matrix products, arithmetic and copies ran while one was open for 0% of the time, Pallas kernels for 6%

profile of v4, /device:TPU:0, one launch (start us, length us, event | category | flops | bytes accessed | tf_op | source)
XLA Modules:
  0.0 39.1 jit_solution(17418394644022390232)
XLA Ops:
  0.6 2.2 %shard_map.113 = bf16[16,80,128]{2,1,0:T(8,128)(2,1)} custom-call(bf16[8,128,128]{2,1,0:T(8,128)(2,1)} %x_hbm.1, f32[1,128]{1,0:T(1,128)} %bitcast.10, bf16[4,128]{1,0:T(4,128)(2,1)} %bitcast.15), custom_call_target="tpu_custom_call" | custom-call | tf_op jit(solution)/shard_map/pallas_call | solution.py:316
  2.8 0.0 copy-start
  2.8 0.0 copy-start.1
  2.8 0.0 copy-start.2
  2.8 0.0 copy-start.5
  2.9 0.0 copy-start.6
  2.9 0.0 copy-start.7
  2.9 7.5 %all-to-all-start = ((bf16[16,80,128]{2,1,0:T(8,128)(2,1)}), bf16[16,80,128]{2,1,0:T(8,128)(2,1)S(1)}, u32[]{:S(2)}, u32[]{:S(2)}) async-start(bf16[16,80,128]{2,1,0:T(8,128)(2,1)} %shard_map.113), calls=%async_computation | async-start | bytes 655360 | tf_op jit(solution)/shard_map/all_to_all | solution.py:332
  10.4 0.0 copy-start.3
  10.4 0.0 copy-start.4
  10.4 0.0 copy-done
  10.5 0.0 copy-done.1
  10.5 0.6 %copy-done.3 = f32[128]{0:T(128)S(1)} copy-done((f32[128]{0:T(128)S(1)}, f32[128]{0:T(128)}, u32[]{:S(2)}) %copy-start.3) | copy-done | bytes 536
  11.1 0.0 copy-done.4
  11.1 0.9 %shard_map.114 = (f32[4,128,128]{2,1,0:T(8,128)S(1)}, bf16[384,128]{1,0:T(8,128)(2,1)S(1)}, bf16[256,256]{1,0:T(8,128)(2,1)S(1)}, f32[64,128]{1,0:T(8,128)S(1)},...) custom-call(s32[1,128]{1,0:T(1,128)S(1)} %bitcast.12, s32[1,128]{1,0:T(1,128)S(1)} %bitcast.13, ...), custom_call_target="tpu_custom_call" | custom-call | tf_op jit(solution)/shard_map/pallas_call | solution.py:316
  12.1 9.5 %all-to-all-done.recv_ref = bf16[16,80,128]{2,1,0:T(8,128)(2,1)S(1)} async-done(((bf16[16,80,128]{2,1,0:T(8,128)(2,1)}), bf16[16,80,128]{2,1,0:T(8,128)(2,1)S(1)}, u32[]{:S(2)}, u32[]{:S(2)}) %all-to-all-start) | async-done | bytes 327712 | tf_op jit(solution)/shard_map/all_to_all | solution.py:332
  21.5 0.1 collective-permute-start
  21.6 1.2 %shard_map.115 = (bf16[8,128,128]{2,1,0:T(8,128)(2,1)S(1)}, bf16[8,1,128,256]{3,2,1,0:T(8,128)(2,1)S(1)}, bf16[8,128,128]{2,1,0:T(8,128)(2,1)S(1)}, bf16[8,64,12...) custom-call(bf16[16,80,128]{2,1,0:T(8,128)(2,1)S(1)} %all-to-all-done.recv_ref, ...), custom_call_target="tpu_custom_call" | custom-call | tf_op jit(solution)/shard_map/pallas_call | solution.py:316
  22.9 0.0 collective-permute-done.other_ref
  22.9 1.7 %shard_map.116 = (bf16[16,64,128]{2,1,0:T(8,128)(2,1)}, bf16[8,128,128]{2,1,0:T(8,128)(2,1)S(1)}) custom-call(bf16[16,16,128]{2,1,0:T(8,128)(2,1)S(1)} %collective-permute-done.other_ref, f32[4,128,128]{2,1,0:T(8,128)S(1)} %get-tuple-element.37.term_ref, bf16[256,256]{1,0:T(8,128)(2,1)S(1)} %get-tuple-element.38.wo_ref, ...), custom_call_target="tpu_custom_call" | custom-call | tf_op jit(solution)/shard_map/pallas_call | solution.py:316
  24.6 3.5 %all-to-all-start.1 = ((bf16[16,64,128]{2,1,0:T(8,128)(2,1)}), bf16[16,64,128]{2,1,0:T(8,128)(2,1)S(1)}, u32[]{:S(2)}, u32[]{:S(2)}) async-start(bf16[16,64,128]{2,1,0:T(8,128)(2,1)} %get-tuple-element.48), calls=%async_computation.1 | async-start | bytes 524288 | tf_op jit(solution)/shard_map/all_to_all | solution.py:332
  28.1 0.2 shard_map.117.mirror_ref
  28.3 9.8 %all-to-all-done.1.recv_ref = bf16[16,64,128]{2,1,0:T(8,128)(2,1)S(1)} async-done(((bf16[16,64,128]{2,1,0:T(8,128)(2,1)}), bf16[16,64,128]{2,1,0:T(8,128)(2,1)S(1)}, u32[]{:S(2)}, u32[]{:S(2)}) %all-to-all-start.1) | async-done | bytes 262176 | tf_op jit(solution)/shard_map/all_to_all | solution.py:332
  38.1 1.0 %shard_map.118 = (bf16[8,128,128]{2,1,0:T(8,128)(2,1)}, bf16[8,64,128]{2,1,0:T(8,128)(2,1)}) custom-call(bf16[16,64,128]{2,1,0:T(8,128)(2,1)S(1)} %all-to-all-done.1.recv_ref, bf16[8,64,128]{2,1,0:T(8,128)(2,1)S(1)} %shard_map.117.mirror_ref, bf16[64,128]{1,0:T(8,128)(2,1)S(1)} %get-tuple-element.50.wd_ref, f32[64,128]{1,0:T(8,128)S(1)} %get-tuple-element.51.db_ref), custom_call_target="tpu_custom_call" | custom-call | tf_op jit(solution)/shard_map/pallas_call | solution.py:316
  (5 shorter events, 0.0 us)
Async XLA Ops:
  2.8 7.6 %copy-start = (bf16[128,4,128]{2,1,0:T(4,128)(2,1)S(1)}, bf16[128,4,128]{2,1,0:T(4,128)(2,1)}, u32[]{:S(2)}) copy-start(bf16[128,4,128]{2,1,0:T(4,128)(2,1)} %w_ref.1) | copy-start | bytes 393220
  2.8 7.6 %copy-start.1 = (bf16[4,32,128]{2,1,0:T(8,128)(2,1)S(1)}, bf16[4,32,128]{2,1,0:T(8,128)(2,1)}, u32[]{:S(2)}) copy-start(bf16[4,32,128]{2,1,0:T(8,128)(2,1)} %param.17) | copy-start | bytes 98308
  2.8 7.6 %copy-start.2 = (bf16[128,64]{0,1:T(8,128)(2,1)S(1)}, bf16[128,64]{0,1:T(8,128)(2,1)}, u32[]{:S(2)}) copy-start(bf16[128,64]{0,1:T(8,128)(2,1)} %param.18) | copy-start | bytes 49156
  2.8 7.6 %copy-start.5 = (s32[128]{0:T(128)S(1)}, s32[128]{0:T(128)}, u32[]{:S(2)}) copy-start(s32[128]{0:T(128)} %param.11) | copy-start | bytes 1540
  2.9 7.6 %copy-start.6 = (s32[128]{0:T(128)S(1)}, s32[128]{0:T(128)}, u32[]{:S(2)}) copy-start(s32[128]{0:T(128)} %param.12) | copy-start | bytes 1540
  2.9 7.6 %copy-start.7 = (f32[64]{0:T(128)S(1)}, f32[64]{0:T(128)}, u32[]{:S(2)}) copy-start(f32[64]{0:T(128)} %param.19) | copy-start | bytes 772
  2.9 18.6 %all-to-all-start = ((bf16[16,80,128]{2,1,0:T(8,128)(2,1)}), bf16[16,80,128]{2,1,0:T(8,128)(2,1)S(1)}, u32[]{:S(2)}, u32[]{:S(2)}) async-start(bf16[16,80,128]{2,1,0:T(8,128)(2,1)} %shard_map.113), calls=%async_computation | async-start | bytes 655360 | tf_op jit(solution)/shard_map/all_to_all | solution.py:332
  10.4 0.7 %copy-start.3 = (f32[128]{0:T(128)S(1)}, f32[128]{0:T(128)}, u32[]{:S(2)}) copy-start(f32[128]{0:T(128)} %param.13) | copy-start | bytes 1540
  10.4 0.7 %copy-start.4 = (f32[2,4]{1,0:T(2,128)S(1)}, f32[2,4]{1,0:T(2,128)}, u32[]{:S(2)}) copy-start(f32[2,4]{1,0:T(2,128)} %cb_ref.1) | copy-start | bytes 100
  21.5 1.4 %collective-permute-start = (bf16[16,16,128]{2,1,0:T(8,128)(2,1)S(1)}, bf16[16,16,128]{2,1,0:T(8,128)(2,1)S(1)}, u32[]{:S(2)}, u32[]{:S(2)}) collective-permute-start(bf16[16,16,128]{2,1,0:T(8,128)(2,1)S(1)} %slice.3), channel_id=1, source_target_pairs={{0,1},{1,0},{2,3},{3,2},{4,5},{5,4},{6,7},{7,6},{8,9},{9,8},{10,11... | collective-permute-start | bytes 196616 | tf_op jit(solution)/shard_map/ppermute | solution.py:328
  24.6 13.5 %all-to-all-start.1 = ((bf16[16,64,128]{2,1,0:T(8,128)(2,1)}), bf16[16,64,128]{2,1,0:T(8,128)(2,1)S(1)}, u32[]{:S(2)}, u32[]{:S(2)}) async-start(bf16[16,64,128]{2,1,0:T(8,128)(2,1)} %get-tuple-element.48), calls=%async_computation.1 | async-start | bytes 524288 | tf_op jit(solution)/shard_map/all_to_all | solution.py:332

commit v5 on v2

--- a/solution.py
+++ b/solution.py
@@ -142,11 +142,11 @@
                 bias_ref[h, at, cs] = extra[start : start + rows] + term_ref[first + h, at, cs]
 
 
-def soften(j, t, keys, spread, bias_ref, scaling, inv_s, e_s):
+def soften(j, t, keys, spread, bias_ref, inv_s, e_s):
     scores = dot_nn(keys, spread)
     for h in range(bias_ref.shape[0]):
         cs = slice(h * LANES, (h + 1) * LANES)
-        s = scores[:, cs] * scaling + bias_ref[h, :, t * LANES : (t + 1) * LANES]
+        s = scores[:, cs] + bias_ref[h, :, t * LANES : (t + 1) * LANES]
         e = jnp.exp2(s - jnp.max(s, 0, keepdims=True))
         inv_s[j, t, h : h + 1] = 1.0 / jnp.sum(e, 0, keepdims=True)
         e_s[j, t, :, cs] = e.astype(BF16)
@@ -210,9 +210,11 @@
     unpack_bias([recv_ref[s, base:] for s in range(peers)], term_ref, 0, bias_s)
     w_qvg = w_ref[...]
     zero = jnp.zeros((dim, LANES), BF16)
+    scaling = dim ** (-0.5) * LOG2E
 
     def project(pair):
-        both = dot_nt(w_qvg, n_s[pl.ds(2 * pair, 2)].reshape(2 * n, chan)).astype(BF16)
+        both = dot_nt(w_qvg, n_s[pl.ds(2 * pair, 2)].reshape(2 * n, chan))
+        both = jnp.concatenate([both[:width] * scaling, both[width:]], 0).astype(BF16)
         for side in range(2):
             j = 2 * pair + side
             qvg = both[:, side * n : (side + 1) * n]
@@ -223,13 +225,12 @@
                 for h in range(heads):
                     target = (own_spread, spread_s)[h // half]
                     cs = slice(h % half * LANES, (h % half + 1) * LANES)
-                    for other in range(heads):
+                    for other in range(half if h < half else heads):
                         block = qvg[h * dim : (h + 1) * dim, t * LANES : (t + 1) * LANES] if h == other else zero
                         target[j, t, other * dim : (other + 1) * dim, cs] = block
 
-    scaling = dim ** (-0.5) * LOG2E
     for_each(rows // 2, tiles, project)
-    for_each(rows, tiles, lambda j: [soften(j, t, k_s[j], own_spread[j, t], bias_s, scaling, inv_s, e_s) for t in range(tiles)])
+    for_each(rows, tiles, lambda j: [soften(j, t, k_s[j, :, :part], own_spread[j, t], bias_s, inv_s, e_s) for t in range(tiles)])
     for_each(rows, tiles, lambda j: [combine(j, t, own_v[j], own_g[j], inv_s, e_s, gated_ref) for t in range(tiles)])
 
 
@@ -245,12 +246,11 @@
     peers = other_ref.shape[0]
     rows, n, chan = x_s.shape
     tiles = n // LANES
-    half, part = bias_s.shape[0], v_s.shape[1]
-    scaling = (part // half) ** (-0.5) * LOG2E
+    half = bias_s.shape[0]
     w_out = wo_ref[...]
 
     unpack_bias([other_ref[s] for s in range(peers)], term_ref, half, bias_s)
-    for_each(rows, tiles, lambda j: [soften(j, t, k_s[j], spread_s[j, t], bias_s, scaling, inv_s, e_s) for t in range(tiles)])
+    for_each(rows, tiles, lambda j: [soften(j, t, k_s[j], spread_s[j, t], bias_s, inv_s, e_s) for t in range(tiles)])
     for_each(rows, tiles, lambda j: [combine(j, t, v_s[j], g_s[j], inv_s, e_s, gated_s) for t in range(tiles)])
 
     def updated(pair):
@@ -396,7 +396,8 @@
         [received, gain, w_types, w_keys, term],
         scratch=[
             pltpu.VMEM((rows, n, chan), BF16),
-            *(pltpu.VMEM(*shape) for shape in (spread_shape, values_shape, gates_shape)),
+            pltpu.VMEM((rows, tiles, width // 2, heads // 2 * LANES), BF16),
+            *(pltpu.VMEM(*shape) for shape in (values_shape, gates_shape)),
             *softmax_scratch,
         ],
     )

time: 38.6 us -> 38.5 us (level)
  no operation moved by 1% of the time
where the time goes in v5:
time: 38.5 us; the launch traced here: 38.2 us
  blocking collectives  13.2 us (34%)
  waiting for transfers between devices  9.46 us (25%)
  starting transfers between devices  7.64 us (20%)
  Pallas kernels  6.36 us (17%)
  between operations  0.78 us (2%)
  local copies, waits for them, and re-layouts  0.66 us (2%)
    all_to_all x1, blocking collectives, all_to_all(): lax.all_to_all(blocks, 'row', split_axis=0, concat_axis=0, tiled=True)  13.2 us
    all_to_all x1, waiting for transfers between devices, all_to_all(): lax.all_to_all(blocks, 'row', split_axis=0, concat_axis=0, tiled=True)  9.46 us
    all_to_all x1, starting transfers between devices, all_to_all(): lax.all_to_all(blocks, 'row', split_axis=0, concat_axis=0, tiled=True)  7.53 us
    pallas_call x5, Pallas kernels, call(): pl.pallas_call(kernel, out_shape=[jax.ShapeDtypeStruct(s, d) for s, d in...  6.36 us
  transfers between devices with their start and end apart: 2, of which 1 were waited for; matrix products, arithmetic and copies ran while one was open for 0% of the time, Pallas kernels for 6%

profile of v5, /device:TPU:0, one launch (start us, length us, event | category | flops | bytes accessed | tf_op | source)
XLA Modules:
  0.0 38.2 jit_solution(7730599256143633487)
XLA Ops:
  0.6 2.2 %shard_map.113 = bf16[16,80,128]{2,1,0:T(8,128)(2,1)} custom-call(bf16[8,128,128]{2,1,0:T(8,128)(2,1)} %x_hbm.1, f32[1,128]{1,0:T(1,128)} %bitcast.10, bf16[4,128]{1,0:T(4,128)(2,1)} %bitcast.15), custom_call_target="tpu_custom_call" | custom-call | tf_op jit(solution)/shard_map/pallas_call | solution.py:313
  2.8 0.0 copy-start
  2.8 0.0 copy-start.1
  2.8 0.0 copy-start.2
  2.8 0.0 copy-start.5
  2.8 0.0 copy-start.6
  2.9 0.0 copy-start.7
  2.9 7.5 %all-to-all-start = ((bf16[16,80,128]{2,1,0:T(8,128)(2,1)}), bf16[16,80,128]{2,1,0:T(8,128)(2,1)S(1)}, u32[]{:S(2)}, u32[]{:S(2)}) async-start(bf16[16,80,128]{2,1,0:T(8,128)(2,1)} %shard_map.113), calls=%async_computation | async-start | bytes 655360 | tf_op jit(solution)/shard_map/all_to_all | solution.py:329
  10.4 0.0 copy-start.3
  10.4 0.0 copy-start.4
  10.4 0.0 copy-done
  10.4 0.0 copy-done.1
  10.5 0.0 copy-done.2
  10.5 0.0 copy-done.5
  10.5 0.6 %copy-done.3 = f32[128]{0:T(128)S(1)} copy-done((f32[128]{0:T(128)S(1)}, f32[128]{0:T(128)}, u32[]{:S(2)}) %copy-start.3) | copy-done | bytes 536
  11.1 0.0 copy-done.4
  11.1 0.9 %shard_map.114 = (f32[4,128,128]{2,1,0:T(8,128)S(1)}, bf16[384,128]{1,0:T(8,128)(2,1)S(1)}, bf16[256,256]{1,0:T(8,128)(2,1)S(1)}, f32[64,128]{1,0:T(8,128)S(1)},...) custom-call(s32[1,128]{1,0:T(1,128)S(1)} %bitcast.12, s32[1,128]{1,0:T(1,128)S(1)} %bitcast.13, ...), custom_call_target="tpu_custom_call" | custom-call | tf_op jit(solution)/shard_map/pallas_call | solution.py:313
  12.0 9.5 %all-to-all-done.recv_ref = bf16[16,80,128]{2,1,0:T(8,128)(2,1)S(1)} async-done(((bf16[16,80,128]{2,1,0:T(8,128)(2,1)}), bf16[16,80,128]{2,1,0:T(8,128)(2,1)S(1)}, u32[]{:S(2)}, u32[]{:S(2)}) %all-to-all-start) | async-done | bytes 327712 | tf_op jit(solution)/shard_map/all_to_all | solution.py:329
  21.5 0.1 collective-permute-start
  21.6 1.2 %shard_map.115 = (bf16[8,128,128]{2,1,0:T(8,128)(2,1)S(1)}, bf16[8,1,128,256]{3,2,1,0:T(8,128)(2,1)S(1)}, bf16[8,128,128]{2,1,0:T(8,128)(2,1)S(1)}, bf16[8,64,12...) custom-call(bf16[16,80,128]{2,1,0:T(8,128)(2,1)S(1)} %all-to-all-done.recv_ref, ...), custom_call_target="tpu_custom_call" | custom-call | tf_op jit(solution)/shard_map/pallas_call | solution.py:313
  22.8 0.0 collective-permute-done.other_ref
  22.8 1.1 %shard_map.116 = (bf16[16,64,128]{2,1,0:T(8,128)(2,1)S(1)}, bf16[8,64,128]{2,1,0:T(8,128)(2,1)S(1)}) custom-call(bf16[16,16,128]{2,1,0:T(8,128)(2,1)S(1)} %collective-permute-done.other_ref, f32[4,128,128]{2,1,0:T(8,128)S(1)} %get-tuple-element.35.term_ref, bf16[256,256]{1,0:T(8,128)(2,1)S(1)} %get-tuple-element.36.wo_ref, ...), custom_call_target="tpu_custom_call" | custom-call | tf_op jit(solution)/shard_map/pallas_call | solution.py:313
  24.0 13.2 %all_to_all.10.recv_ref = bf16[16,64,128]{2,1,0:T(8,128)(2,1)S(1)} all-to-all(bf16[16,64,128]{2,1,0:T(8,128)(2,1)S(1)} %get-tuple-element.48), channel_id=1, replica_groups=mesh['dp'=2,'head'=1,'row'=16] {'row'}, dimensions={0} | all-to-all | bytes 524288 | tf_op jit(solution)/shard_map/all_to_all | solution.py:329
  37.2 1.0 %shard_map.117 = (bf16[8,128,128]{2,1,0:T(8,128)(2,1)}, bf16[8,64,128]{2,1,0:T(8,128)(2,1)}) custom-call(bf16[16,64,128]{2,1,0:T(8,128)(2,1)S(1)} %all_to_all.10.recv_ref, bf16[8,64,128]{2,1,0:T(8,128)(2,1)S(1)} %get-tuple-element.49.mirror_ref, bf16[64,128]{1,0:T(8,128)(2,1)S(1)} %get-tuple-element.37.wd_ref, f32[64,128]{1,0:T(8,128)S(1)} %get-tuple-element.38.db_ref), custom_call_target="tpu_custom_call" | custom-call | tf_op jit(solution)/shard_map/pallas_call | solution.py:313
  (3 shorter events, 0.0 us)
Async XLA Ops:
  2.8 7.6 %copy-start = (bf16[128,4,128]{2,1,0:T(4,128)(2,1)S(1)}, bf16[128,4,128]{2,1,0:T(4,128)(2,1)}, u32[]{:S(2)}) copy-start(bf16[128,4,128]{2,1,0:T(4,128)(2,1)} %w_ref.1) | copy-start | bytes 393220
  2.8 7.6 %copy-start.1 = (bf16[4,32,128]{2,1,0:T(8,128)(2,1)S(1)}, bf16[4,32,128]{2,1,0:T(8,128)(2,1)}, u32[]{:S(2)}) copy-start(bf16[4,32,128]{2,1,0:T(8,128)(2,1)} %param.17) | copy-start | bytes 98308
  2.8 7.6 %copy-start.2 = (bf16[128,64]{0,1:T(8,128)(2,1)S(1)}, bf16[128,64]{0,1:T(8,128)(2,1)}, u32[]{:S(2)}) copy-start(bf16[128,64]{0,1:T(8,128)(2,1)} %param.18) | copy-start | bytes 49156
  2.8 7.6 %copy-start.5 = (s32[128]{0:T(128)S(1)}, s32[128]{0:T(128)}, u32[]{:S(2)}) copy-start(s32[128]{0:T(128)} %param.11) | copy-start | bytes 1540
  2.8 7.6 %copy-start.6 = (s32[128]{0:T(128)S(1)}, s32[128]{0:T(128)}, u32[]{:S(2)}) copy-start(s32[128]{0:T(128)} %param.12) | copy-start | bytes 1540
  2.9 7.6 %copy-start.7 = (f32[64]{0:T(128)S(1)}, f32[64]{0:T(128)}, u32[]{:S(2)}) copy-start(f32[64]{0:T(128)} %param.19) | copy-start | bytes 772
  2.9 18.6 %all-to-all-start = ((bf16[16,80,128]{2,1,0:T(8,128)(2,1)}), bf16[16,80,128]{2,1,0:T(8,128)(2,1)S(1)}, u32[]{:S(2)}, u32[]{:S(2)}) async-start(bf16[16,80,128]{2,1,0:T(8,128)(2,1)} %shard_map.113), calls=%async_computation | async-start | bytes 655360 | tf_op jit(solution)/shard_map/all_to_all | solution.py:329
  10.4 0.7 %copy-start.3 = (f32[128]{0:T(128)S(1)}, f32[128]{0:T(128)}, u32[]{:S(2)}) copy-start(f32[128]{0:T(128)} %param.13) | copy-start | bytes 1540
  10.4 0.7 %copy-start.4 = (f32[2,4]{1,0:T(2,128)S(1)}, f32[2,4]{1,0:T(2,128)}, u32[]{:S(2)}) copy-start(f32[2,4]{1,0:T(2,128)} %cb_ref.1) | copy-start | bytes 100
  21.5 1.3 %collective-permute-start = (bf16[16,16,128]{2,1,0:T(8,128)(2,1)S(1)}, bf16[16,16,128]{2,1,0:T(8,128)(2,1)S(1)}, u32[]{:S(2)}, u32[]{:S(2)}) collective-permute-start(bf16[16,16,128]{2,1,0:T(8,128)(2,1)S(1)} %slice.3), channel_id=1, source_target_pairs={{0,1},{1,0},{2,3},{3,2},{4,5},{5,4},{6,7},{7,6},{8,9},{9,8},{10,11... | collective-permute-start | bytes 196616 | tf_op jit(solution)/shard_map/ppermute | solution.py:325

commit v6 on v2

--- a/solution.py
+++ b/solution.py
@@ -211,8 +211,10 @@
     w_qvg = w_ref[...]
     zero = jnp.zeros((dim, LANES), BF16)
 
-    def project(pair):
-        both = dot_nt(w_qvg, n_s[pl.ds(2 * pair, 2)].reshape(2 * n, chan)).astype(BF16)
+    def product(pair):
+        return dot_nt(w_qvg, n_s[pl.ds(2 * pair, 2)].reshape(2 * n, chan)).astype(BF16)
+
+    def spread_out(pair, both):
         for side in range(2):
             j = 2 * pair + side
             qvg = both[:, side * n : (side + 1) * n]
@@ -228,7 +230,12 @@
                         target[j, t, other * dim : (other + 1) * dim, cs] = block
 
     scaling = dim ** (-0.5) * LOG2E
-    for_each(rows // 2, tiles, project)
+    if tiles == 1:
+        products = [product(pair) for pair in range(rows // 2)]
+        for pair in range(rows // 2):
+            spread_out(pair, products[pair])
+    else:
+        pl.loop(0, rows // 2)(lambda pair: spread_out(pair, product(pair)))
     for_each(rows, tiles, lambda j: [soften(j, t, k_s[j], own_spread[j, t], bias_s, scaling, inv_s, e_s) for t in range(tiles)])
     for_each(rows, tiles, lambda j: [combine(j, t, own_v[j], own_g[j], inv_s, e_s, gated_ref) for t in range(tiles)])
 
@@ -266,8 +273,9 @@
         for_each(rows // 2, tiles, store_update)
         return
 
+    updates = [updated(pair) for pair in range(rows // 2)]
     for j in range(0, rows, 2):
-        update = updated(j // 2).astype(F32)
+        update = updates[j // 2].astype(F32)
         for side in range(2):
             new = (x_s[j + side].astype(F32) + update[:, side * chan : (side + 1) * chan]).astype(BF16)
             new_s[j + side] = new

time: 38.6 us -> 38.6 us (level)
  no operation moved by 1% of the time
where the time goes in v6:
time: 38.6 us; the launch traced here: 38.2 us
  blocking collectives  13.2 us (34%)
  waiting for transfers between devices  9.46 us (25%)
  starting transfers between devices  7.64 us (20%)
  Pallas kernels  6.42 us (17%)
  between operations  0.78 us (2%)
  local copies, waits for them, and re-layouts  0.66 us (2%)
    all_to_all x1, blocking collectives, all_to_all(): lax.all_to_all(blocks, 'row', split_axis=0, concat_axis=0, tiled=True)  13.2 us
    all_to_all x1, waiting for transfers between devices, all_to_all(): lax.all_to_all(blocks, 'row', split_axis=0, concat_axis=0, tiled=True)  9.46 us
    all_to_all x1, starting transfers between devices, all_to_all(): lax.all_to_all(blocks, 'row', split_axis=0, concat_axis=0, tiled=True)  7.53 us
    pallas_call x5, Pallas kernels, call(): pl.pallas_call(kernel, out_shape=[jax.ShapeDtypeStruct(s, d) for s, d in...  6.42 us
  transfers between devices with their start and end apart: 2, of which 1 were waited for; matrix products, arithmetic and copies ran while one was open for 0% of the time, Pallas kernels for 6%

profile of v6, /device:TPU:0, one launch (start us, length us, event | category | flops | bytes accessed | tf_op | source)
XLA Modules:
  0.0 38.2 jit_solution(5971858968319037375)
XLA Ops:
  0.6 2.2 %shard_map.113 = bf16[16,80,128]{2,1,0:T(8,128)(2,1)} custom-call(bf16[8,128,128]{2,1,0:T(8,128)(2,1)} %x_hbm.1, f32[1,128]{1,0:T(1,128)} %bitcast.10, bf16[4,128]{1,0:T(4,128)(2,1)} %bitcast.15), custom_call_target="tpu_custom_call" | custom-call | tf_op jit(solution)/shard_map/pallas_call | solution.py:321
  2.8 0.0 copy-start
  2.8 0.0 copy-start.1
  2.8 0.0 copy-start.2
  2.8 0.0 copy-start.5
  2.8 0.0 copy-start.6
  2.9 0.0 copy-start.7
  2.9 7.5 %all-to-all-start = ((bf16[16,80,128]{2,1,0:T(8,128)(2,1)}), bf16[16,80,128]{2,1,0:T(8,128)(2,1)S(1)}, u32[]{:S(2)}, u32[]{:S(2)}) async-start(bf16[16,80,128]{2,1,0:T(8,128)(2,1)} %shard_map.113), calls=%async_computation | async-start | bytes 655360 | tf_op jit(solution)/shard_map/all_to_all | solution.py:337
  10.4 0.0 copy-start.3
  10.4 0.0 copy-start.4
  10.4 0.0 copy-done
  10.4 0.0 copy-done.1
  10.5 0.0 copy-done.2
  10.5 0.0 copy-done.5
  10.5 0.6 %copy-done.3 = f32[128]{0:T(128)S(1)} copy-done((f32[128]{0:T(128)S(1)}, f32[128]{0:T(128)}, u32[]{:S(2)}) %copy-start.3) | copy-done | bytes 536
  11.1 0.0 copy-done.4
  11.1 0.9 %shard_map.114 = (f32[4,128,128]{2,1,0:T(8,128)S(1)}, bf16[384,128]{1,0:T(8,128)(2,1)S(1)}, bf16[256,256]{1,0:T(8,128)(2,1)S(1)}, f32[64,128]{1,0:T(8,128)S(1)},...) custom-call(s32[1,128]{1,0:T(1,128)S(1)} %bitcast.12, s32[1,128]{1,0:T(1,128)S(1)} %bitcast.13, ...), custom_call_target="tpu_custom_call" | custom-call | tf_op jit(solution)/shard_map/pallas_call | solution.py:321
  12.0 9.5 %all-to-all-done.recv_ref = bf16[16,80,128]{2,1,0:T(8,128)(2,1)S(1)} async-done(((bf16[16,80,128]{2,1,0:T(8,128)(2,1)}), bf16[16,80,128]{2,1,0:T(8,128)(2,1)S(1)}, u32[]{:S(2)}, u32[]{:S(2)}) %all-to-all-start) | async-done | bytes 327712 | tf_op jit(solution)/shard_map/all_to_all | solution.py:337
  21.5 0.1 collective-permute-start
  21.6 1.2 %shard_map.115 = (bf16[8,128,128]{2,1,0:T(8,128)(2,1)S(1)}, bf16[8,1,128,256]{3,2,1,0:T(8,128)(2,1)S(1)}, bf16[8,128,128]{2,1,0:T(8,128)(2,1)S(1)}, bf16[8,64,12...) custom-call(bf16[16,80,128]{2,1,0:T(8,128)(2,1)S(1)} %all-to-all-done.recv_ref, ...), custom_call_target="tpu_custom_call" | custom-call | tf_op jit(solution)/shard_map/pallas_call | solution.py:321
  22.9 0.0 collective-permute-done.other_ref
  22.9 1.1 %shard_map.116 = (bf16[16,64,128]{2,1,0:T(8,128)(2,1)S(1)}, bf16[8,64,128]{2,1,0:T(8,128)(2,1)S(1)}) custom-call(bf16[16,16,128]{2,1,0:T(8,128)(2,1)S(1)} %collective-permute-done.other_ref, f32[4,128,128]{2,1,0:T(8,128)S(1)} %get-tuple-element.35.term_ref, bf16[256,256]{1,0:T(8,128)(2,1)S(1)} %get-tuple-element.36.wo_ref, ...), custom_call_target="tpu_custom_call" | custom-call | tf_op jit(solution)/shard_map/pallas_call | solution.py:321
  24.0 13.2 %all_to_all.10.recv_ref = bf16[16,64,128]{2,1,0:T(8,128)(2,1)S(1)} all-to-all(bf16[16,64,128]{2,1,0:T(8,128)(2,1)S(1)} %get-tuple-element.48), channel_id=1, replica_groups=mesh['dp'=2,'head'=1,'row'=16] {'row'}, dimensions={0} | all-to-all | bytes 524288 | tf_op jit(solution)/shard_map/all_to_all | solution.py:337
  37.3 1.0 %shard_map.117 = (bf16[8,128,128]{2,1,0:T(8,128)(2,1)}, bf16[8,64,128]{2,1,0:T(8,128)(2,1)}) custom-call(bf16[16,64,128]{2,1,0:T(8,128)(2,1)S(1)} %all_to_all.10.recv_ref, bf16[8,64,128]{2,1,0:T(8,128)(2,1)S(1)} %get-tuple-element.49.mirror_ref, bf16[64,128]{1,0:T(8,128)(2,1)S(1)} %get-tuple-element.37.wd_ref, f32[64,128]{1,0:T(8,128)S(1)} %get-tuple-element.38.db_ref), custom_call_target="tpu_custom_call" | custom-call | tf_op jit(solution)/shard_map/pallas_call | solution.py:321
  (3 shorter events, 0.0 us)
Async XLA Ops:
  2.8 7.6 %copy-start = (bf16[128,4,128]{2,1,0:T(4,128)(2,1)S(1)}, bf16[128,4,128]{2,1,0:T(4,128)(2,1)}, u32[]{:S(2)}) copy-start(bf16[128,4,128]{2,1,0:T(4,128)(2,1)} %w_ref.1) | copy-start | bytes 393220
  2.8 7.6 %copy-start.1 = (bf16[4,32,128]{2,1,0:T(8,128)(2,1)S(1)}, bf16[4,32,128]{2,1,0:T(8,128)(2,1)}, u32[]{:S(2)}) copy-start(bf16[4,32,128]{2,1,0:T(8,128)(2,1)} %param.17) | copy-start | bytes 98308
  2.8 7.6 %copy-start.2 = (bf16[128,64]{0,1:T(8,128)(2,1)S(1)}, bf16[128,64]{0,1:T(8,128)(2,1)}, u32[]{:S(2)}) copy-start(bf16[128,64]{0,1:T(8,128)(2,1)} %param.18) | copy-start | bytes 49156
  2.8 7.6 %copy-start.5 = (s32[128]{0:T(128)S(1)}, s32[128]{0:T(128)}, u32[]{:S(2)}) copy-start(s32[128]{0:T(128)} %param.11) | copy-start | bytes 1540
  2.8 7.6 %copy-start.6 = (s32[128]{0:T(128)S(1)}, s32[128]{0:T(128)}, u32[]{:S(2)}) copy-start(s32[128]{0:T(128)} %param.12) | copy-start | bytes 1540
  2.9 7.6 %copy-start.7 = (f32[64]{0:T(128)S(1)}, f32[64]{0:T(128)}, u32[]{:S(2)}) copy-start(f32[64]{0:T(128)} %param.19) | copy-start | bytes 772
  2.9 18.6 %all-to-all-start = ((bf16[16,80,128]{2,1,0:T(8,128)(2,1)}), bf16[16,80,128]{2,1,0:T(8,128)(2,1)S(1)}, u32[]{:S(2)}, u32[]{:S(2)}) async-start(bf16[16,80,128]{2,1,0:T(8,128)(2,1)} %shard_map.113), calls=%async_computation | async-start | bytes 655360 | tf_op jit(solution)/shard_map/all_to_all | solution.py:337
  10.4 0.7 %copy-start.3 = (f32[128]{0:T(128)S(1)}, f32[128]{0:T(128)}, u32[]{:S(2)}) copy-start(f32[128]{0:T(128)} %param.13) | copy-start | bytes 1540
  10.4 0.7 %copy-start.4 = (f32[2,4]{1,0:T(2,128)S(1)}, f32[2,4]{1,0:T(2,128)}, u32[]{:S(2)}) copy-start(f32[2,4]{1,0:T(2,128)} %cb_ref.1) | copy-start | bytes 100
  21.5 1.4 %collective-permute-start = (bf16[16,16,128]{2,1,0:T(8,128)(2,1)S(1)}, bf16[16,16,128]{2,1,0:T(8,128)(2,1)S(1)}, u32[]{:S(2)}, u32[]{:S(2)}) collective-permute-start(bf16[16,16,128]{2,1,0:T(8,128)(2,1)S(1)} %slice.3), channel_id=1, source_target_pairs={{0,1},{1,0},{2,3},{3,2},{4,5},{5,4},{6,7},{7,6},{8,9},{9,8},{10,11... | collective-permute-start | bytes 196616 | tf_op jit(solution)/shard_map/ppermute | solution.py:333

commit v7 on v2

--- a/solution.py
+++ b/solution.py
@@ -297,13 +297,16 @@
             at = pl.ds((pair + 1 - share) * group, share * group)
             copies.append(pltpu.make_async_copy(new_ref.at[:, at, :], new_hbm.at[:, at, :], sems.at[len(copies)]))
             copies[-1].start()
-    logits_of(new_ref, wd_ref[...], db_ref[:, :1], dist_ref)
-    for i in range(rows):
-        dist_ref[i] = (dist_ref[i].astype(F32) + mirror_ref[i].astype(F32)).astype(BF16)
-        if i % 2:
-            at = pl.ds(i - 1, 2)
-            copies.append(pltpu.make_async_copy(dist_ref.at[at], dist_hbm.at[at], sems.at[len(copies)]))
-            copies[-1].start()
+    n, half = new_ref.shape[1], rows // 2
+    for first in range(0, rows, half):
+        block = new_ref[first : first + half].reshape(half * n, chan)
+        logits = dot_nt(wd_ref[...], block) + db_ref[:, :1]
+        for i in range(half):
+            own = logits[:, i * n : (i + 1) * n].astype(BF16).astype(F32)
+            dist_ref[first + i] = (own + mirror_ref[first + i].astype(F32)).astype(BF16)
+        at = pl.ds(first, half)
+        copies.append(pltpu.make_async_copy(dist_ref.at[at], dist_hbm.at[at], sems.at[len(copies)]))
+        copies[-1].start()
     for copy in copies:
         copy.wait()
 
@@ -426,7 +429,7 @@
         scratch=[
             pltpu.VMEM((rows, n, chan), BF16),
             pltpu.VMEM((rows, bins, n), BF16),
-            pltpu.SemaphoreType.DMA((2 + rows // 2,)),
+            pltpu.SemaphoreType.DMA((4,)),
         ],
         hbm_outs=True,
     )

time: 38.6 us -> 38.5 us (level)
  no operation moved by 1% of the time
where the time goes in v7:
time: 38.5 us; the launch traced here: 38.2 us
  blocking collectives  13.2 us (34%)
  waiting for transfers between devices  9.46 us (25%)
  starting transfers between devices  7.64 us (20%)
  Pallas kernels  6.38 us (17%)
  between operations  0.78 us (2%)
  local copies, waits for them, and re-layouts  0.66 us (2%)
    all_to_all x1, blocking collectives, all_to_all(): lax.all_to_all(blocks, 'row', split_axis=0, concat_axis=0, tiled=True)  13.2 us
    all_to_all x1, waiting for transfers between devices, all_to_all(): lax.all_to_all(blocks, 'row', split_axis=0, concat_axis=0, tiled=True)  9.46 us
    all_to_all x1, starting transfers between devices, all_to_all(): lax.all_to_all(blocks, 'row', split_axis=0, concat_axis=0, tiled=True)  7.53 us
    pallas_call x5, Pallas kernels, call(): pl.pallas_call(kernel, out_shape=[jax.ShapeDtypeStruct(s, d) for s, d in...  6.38 us
  transfers between devices with their start and end apart: 2, of which 1 were waited for; matrix products, arithmetic and copies ran while one was open for 0% of the time, Pallas kernels for 6%

profile of v7, /device:TPU:0, one launch (start us, length us, event | category | flops | bytes accessed | tf_op | source)
XLA Modules:
  0.0 38.2 jit_solution(3992199809887050975)
XLA Ops:
  0.6 2.2 %shard_map.113 = bf16[16,80,128]{2,1,0:T(8,128)(2,1)} custom-call(bf16[8,128,128]{2,1,0:T(8,128)(2,1)} %x_hbm.1, f32[1,128]{1,0:T(1,128)} %bitcast.10, bf16[4,128]{1,0:T(4,128)(2,1)} %bitcast.15), custom_call_target="tpu_custom_call" | custom-call | tf_op jit(solution)/shard_map/pallas_call | solution.py:316
  2.8 0.0 copy-start
  2.8 0.0 copy-start.1
  2.8 0.0 copy-start.2
  2.8 0.0 copy-start.5
  2.8 0.0 copy-start.6
  2.9 0.0 copy-start.7
  2.9 7.5 %all-to-all-start = ((bf16[16,80,128]{2,1,0:T(8,128)(2,1)}), bf16[16,80,128]{2,1,0:T(8,128)(2,1)S(1)}, u32[]{:S(2)}, u32[]{:S(2)}) async-start(bf16[16,80,128]{2,1,0:T(8,128)(2,1)} %shard_map.113), calls=%async_computation | async-start | bytes 655360 | tf_op jit(solution)/shard_map/all_to_all | solution.py:332
  10.4 0.0 copy-start.3
  10.4 0.0 copy-start.4
  10.4 0.0 copy-done
  10.4 0.0 copy-done.1
  10.5 0.0 copy-done.2
  10.5 0.0 copy-done.5
  10.5 0.6 %copy-done.3 = f32[128]{0:T(128)S(1)} copy-done((f32[128]{0:T(128)S(1)}, f32[128]{0:T(128)}, u32[]{:S(2)}) %copy-start.3) | copy-done | bytes 536
  11.1 0.0 copy-done.4
  11.1 0.9 %shard_map.114 = (f32[4,128,128]{2,1,0:T(8,128)S(1)}, bf16[384,128]{1,0:T(8,128)(2,1)S(1)}, bf16[256,256]{1,0:T(8,128)(2,1)S(1)}, f32[64,128]{1,0:T(8,128)S(1)},...) custom-call(s32[1,128]{1,0:T(1,128)S(1)} %bitcast.12, s32[1,128]{1,0:T(1,128)S(1)} %bitcast.13, ...), custom_call_target="tpu_custom_call" | custom-call | tf_op jit(solution)/shard_map/pallas_call | solution.py:316
  12.0 9.5 %all-to-all-done.recv_ref = bf16[16,80,128]{2,1,0:T(8,128)(2,1)S(1)} async-done(((bf16[16,80,128]{2,1,0:T(8,128)(2,1)}), bf16[16,80,128]{2,1,0:T(8,128)(2,1)S(1)}, u32[]{:S(2)}, u32[]{:S(2)}) %all-to-all-start) | async-done | bytes 327712 | tf_op jit(solution)/shard_map/all_to_all | solution.py:332
  21.5 0.1 collective-permute-start
  21.6 1.2 %shard_map.115 = (bf16[8,128,128]{2,1,0:T(8,128)(2,1)S(1)}, bf16[8,1,128,256]{3,2,1,0:T(8,128)(2,1)S(1)}, bf16[8,128,128]{2,1,0:T(8,128)(2,1)S(1)}, bf16[8,64,12...) custom-call(bf16[16,80,128]{2,1,0:T(8,128)(2,1)S(1)} %all-to-all-done.recv_ref, ...), custom_call_target="tpu_custom_call" | custom-call | tf_op jit(solution)/shard_map/pallas_call | solution.py:316
  22.9 0.0 collective-permute-done.other_ref
  22.9 1.1 %shard_map.116 = (bf16[16,64,128]{2,1,0:T(8,128)(2,1)S(1)}, bf16[8,64,128]{2,1,0:T(8,128)(2,1)S(1)}) custom-call(bf16[16,16,128]{2,1,0:T(8,128)(2,1)S(1)} %collective-permute-done.other_ref, f32[4,128,128]{2,1,0:T(8,128)S(1)} %get-tuple-element.35.term_ref, bf16[256,256]{1,0:T(8,128)(2,1)S(1)} %get-tuple-element.36.wo_ref, ...), custom_call_target="tpu_custom_call" | custom-call | tf_op jit(solution)/shard_map/pallas_call | solution.py:316
  24.0 13.2 %all_to_all.10.recv_ref = bf16[16,64,128]{2,1,0:T(8,128)(2,1)S(1)} all-to-all(bf16[16,64,128]{2,1,0:T(8,128)(2,1)S(1)} %get-tuple-element.48), channel_id=1, replica_groups=mesh['dp'=2,'head'=1,'row'=16] {'row'}, dimensions={0} | all-to-all | bytes 524288 | tf_op jit(solution)/shard_map/all_to_all | solution.py:332
  37.3 0.9 %shard_map.117 = (bf16[8,128,128]{2,1,0:T(8,128)(2,1)}, bf16[8,64,128]{2,1,0:T(8,128)(2,1)}) custom-call(bf16[16,64,128]{2,1,0:T(8,128)(2,1)S(1)} %all_to_all.10.recv_ref, bf16[8,64,128]{2,1,0:T(8,128)(2,1)S(1)} %get-tuple-element.49.mirror_ref, bf16[64,128]{1,0:T(8,128)(2,1)S(1)} %get-tuple-element.37.wd_ref, f32[64,128]{1,0:T(8,128)S(1)} %get-tuple-element.38.db_ref), custom_call_target="tpu_custom_call" | custom-call | tf_op jit(solution)/shard_map/pallas_call | solution.py:316
  (3 shorter events, 0.0 us)
Async XLA Ops:
  2.8 7.6 %copy-start = (bf16[128,4,128]{2,1,0:T(4,128)(2,1)S(1)}, bf16[128,4,128]{2,1,0:T(4,128)(2,1)}, u32[]{:S(2)}) copy-start(bf16[128,4,128]{2,1,0:T(4,128)(2,1)} %w_ref.1) | copy-start | bytes 393220
  2.8 7.6 %copy-start.1 = (bf16[4,32,128]{2,1,0:T(8,128)(2,1)S(1)}, bf16[4,32,128]{2,1,0:T(8,128)(2,1)}, u32[]{:S(2)}) copy-start(bf16[4,32,128]{2,1,0:T(8,128)(2,1)} %param.17) | copy-start | bytes 98308
  2.8 7.6 %copy-start.2 = (bf16[128,64]{0,1:T(8,128)(2,1)S(1)}, bf16[128,64]{0,1:T(8,128)(2,1)}, u32[]{:S(2)}) copy-start(bf16[128,64]{0,1:T(8,128)(2,1)} %param.18) | copy-start | bytes 49156
  2.8 7.6 %copy-start.5 = (s32[128]{0:T(128)S(1)}, s32[128]{0:T(128)}, u32[]{:S(2)}) copy-start(s32[128]{0:T(128)} %param.11) | copy-start | bytes 1540
  2.8 7.6 %copy-start.6 = (s32[128]{0:T(128)S(1)}, s32[128]{0:T(128)}, u32[]{:S(2)}) copy-start(s32[128]{0:T(128)} %param.12) | copy-start | bytes 1540
  2.9 7.6 %copy-start.7 = (f32[64]{0:T(128)S(1)}, f32[64]{0:T(128)}, u32[]{:S(2)}) copy-start(f32[64]{0:T(128)} %param.19) | copy-start | bytes 772
  2.9 18.6 %all-to-all-start = ((bf16[16,80,128]{2,1,0:T(8,128)(2,1)}), bf16[16,80,128]{2,1,0:T(8,128)(2,1)S(1)}, u32[]{:S(2)}, u32[]{:S(2)}) async-start(bf16[16,80,128]{2,1,0:T(8,128)(2,1)} %shard_map.113), calls=%async_computation | async-start | bytes 655360 | tf_op jit(solution)/shard_map/all_to_all | solution.py:332
  10.4 0.7 %copy-start.3 = (f32[128]{0:T(128)S(1)}, f32[128]{0:T(128)}, u32[]{:S(2)}) copy-start(f32[128]{0:T(128)} %param.13) | copy-start | bytes 1540
  10.4 0.7 %copy-start.4 = (f32[2,4]{1,0:T(2,128)S(1)}, f32[2,4]{1,0:T(2,128)}, u32[]{:S(2)}) copy-start(f32[2,4]{1,0:T(2,128)} %cb_ref.1) | copy-start | bytes 100
  21.5 1.4 %collective-permute-start = (bf16[16,16,128]{2,1,0:T(8,128)(2,1)S(1)}, bf16[16,16,128]{2,1,0:T(8,128)(2,1)S(1)}, u32[]{:S(2)}, u32[]{:S(2)}) collective-permute-start(bf16[16,16,128]{2,1,0:T(8,128)(2,1)S(1)} %slice.3), channel_id=1, source_target_pairs={{0,1},{1,0},{2,3},{3,2},{4,5},{5,4},{6,7},{7,6},{8,9},{9,8},{10,11... | collective-permute-start | bytes 196616 | tf_op jit(solution)/shard_map/ppermute | solution.py:328

commit v8 on v5

--- a/solution.py
+++ b/solution.py
@@ -297,13 +297,16 @@
             at = pl.ds((pair + 1 - share) * group, share * group)
             copies.append(pltpu.make_async_copy(new_ref.at[:, at, :], new_hbm.at[:, at, :], sems.at[len(copies)]))
             copies[-1].start()
-    logits_of(new_ref, wd_ref[...], db_ref[:, :1], dist_ref)
-    for i in range(rows):
-        dist_ref[i] = (dist_ref[i].astype(F32) + mirror_ref[i].astype(F32)).astype(BF16)
-        if i % 2:
-            at = pl.ds(i - 1, 2)
-            copies.append(pltpu.make_async_copy(dist_ref.at[at], dist_hbm.at[at], sems.at[len(copies)]))
-            copies[-1].start()
+    n, half = new_ref.shape[1], rows // 2
+    for first in range(0, rows, half):
+        block = new_ref[first : first + half].reshape(half * n, chan)
+        logits = dot_nt(wd_ref[...], block) + db_ref[:, :1]
+        for i in range(half):
+            own = logits[:, i * n : (i + 1) * n].astype(BF16).astype(F32)
+            dist_ref[first + i] = (own + mirror_ref[first + i].astype(F32)).astype(BF16)
+        at = pl.ds(first, half)
+        copies.append(pltpu.make_async_copy(dist_ref.at[at], dist_hbm.at[at], sems.at[len(copies)]))
+        copies[-1].start()
     for copy in copies:
         copy.wait()
 
@@ -427,7 +430,7 @@
         scratch=[
             pltpu.VMEM((rows, n, chan), BF16),
             pltpu.VMEM((rows, bins, n), BF16),
-            pltpu.SemaphoreType.DMA((2 + rows // 2,)),
+            pltpu.SemaphoreType.DMA((4,)),
         ],
         hbm_outs=True,
     )

time: 38.5 us -> 38.5 us (level)
  no operation moved by 1% of the time
where the time goes in v8:
time: 38.5 us; the launch traced here: 38.1 us
  blocking collectives  13.2 us (34%)
  waiting for transfers between devices  9.46 us (25%)
  starting transfers between devices  7.64 us (20%)
  Pallas kernels  6.32 us (16%)
  between operations  0.78 us (2%)
  local copies, waits for them, and re-layouts  0.66 us (2%)
    all_to_all x1, blocking collectives, all_to_all(): lax.all_to_all(blocks, 'row', split_axis=0, concat_axis=0, tiled=True)  13.2 us
    all_to_all x1, waiting for transfers between devices, all_to_all(): lax.all_to_all(blocks, 'row', split_axis=0, concat_axis=0, tiled=True)  9.46 us
    all_to_all x1, starting transfers between devices, all_to_all(): lax.all_to_all(blocks, 'row', split_axis=0, concat_axis=0, tiled=True)  7.53 us
    pallas_call x5, Pallas kernels, call(): pl.pallas_call(kernel, out_shape=[jax.ShapeDtypeStruct(s, d) for s, d in...  6.32 us
  transfers between devices with their start and end apart: 2, of which 1 were waited for; matrix products, arithmetic and copies ran while one was open for 0% of the time, Pallas kernels for 6%

profile of v8, /device:TPU:0, one launch (start us, length us, event | category | flops | bytes accessed | tf_op | source)
XLA Modules:
  0.0 38.1 jit_solution(5312922805871403595)
XLA Ops:
  0.6 2.2 %shard_map.113 = bf16[16,80,128]{2,1,0:T(8,128)(2,1)} custom-call(bf16[8,128,128]{2,1,0:T(8,128)(2,1)} %x_hbm.1, f32[1,128]{1,0:T(1,128)} %bitcast.10, bf16[4,128]{1,0:T(4,128)(2,1)} %bitcast.15), custom_call_target="tpu_custom_call" | custom-call | tf_op jit(solution)/shard_map/pallas_call | solution.py:316
  2.8 0.0 copy-start
  2.8 0.0 copy-start.1
  2.8 0.0 copy-start.2
  2.8 0.0 copy-start.5
  2.8 0.0 copy-start.6
  2.9 0.0 copy-start.7
  2.9 7.5 %all-to-all-start = ((bf16[16,80,128]{2,1,0:T(8,128)(2,1)}), bf16[16,80,128]{2,1,0:T(8,128)(2,1)S(1)}, u32[]{:S(2)}, u32[]{:S(2)}) async-start(bf16[16,80,128]{2,1,0:T(8,128)(2,1)} %shard_map.113), calls=%async_computation | async-start | bytes 655360 | tf_op jit(solution)/shard_map/all_to_all | solution.py:332
  10.4 0.0 copy-start.3
  10.4 0.0 copy-start.4
  10.4 0.0 copy-done
  10.4 0.0 copy-done.1
  10.5 0.0 copy-done.2
  10.5 0.0 copy-done.5
  10.5 0.6 %copy-done.3 = f32[128]{0:T(128)S(1)} copy-done((f32[128]{0:T(128)S(1)}, f32[128]{0:T(128)}, u32[]{:S(2)}) %copy-start.3) | copy-done | bytes 536
  11.1 0.0 copy-done.4
  11.1 0.9 %shard_map.114 = (f32[4,128,128]{2,1,0:T(8,128)S(1)}, bf16[384,128]{1,0:T(8,128)(2,1)S(1)}, bf16[256,256]{1,0:T(8,128)(2,1)S(1)}, f32[64,128]{1,0:T(8,128)S(1)},...) custom-call(s32[1,128]{1,0:T(1,128)S(1)} %bitcast.12, s32[1,128]{1,0:T(1,128)S(1)} %bitcast.13, ...), custom_call_target="tpu_custom_call" | custom-call | tf_op jit(solution)/shard_map/pallas_call | solution.py:316
  12.0 9.5 %all-to-all-done.recv_ref = bf16[16,80,128]{2,1,0:T(8,128)(2,1)S(1)} async-done(((bf16[16,80,128]{2,1,0:T(8,128)(2,1)}), bf16[16,80,128]{2,1,0:T(8,128)(2,1)S(1)}, u32[]{:S(2)}, u32[]{:S(2)}) %all-to-all-start) | async-done | bytes 327712 | tf_op jit(solution)/shard_map/all_to_all | solution.py:332
  21.5 0.1 collective-permute-start
  21.6 1.2 %shard_map.115 = (bf16[8,128,128]{2,1,0:T(8,128)(2,1)S(1)}, bf16[8,1,128,256]{3,2,1,0:T(8,128)(2,1)S(1)}, bf16[8,128,128]{2,1,0:T(8,128)(2,1)S(1)}, bf16[8,64,12...) custom-call(bf16[16,80,128]{2,1,0:T(8,128)(2,1)S(1)} %all-to-all-done.recv_ref, ...), custom_call_target="tpu_custom_call" | custom-call | tf_op jit(solution)/shard_map/pallas_call | solution.py:316
  22.8 0.0 collective-permute-done.other_ref
  22.8 1.1 %shard_map.116 = (bf16[16,64,128]{2,1,0:T(8,128)(2,1)S(1)}, bf16[8,64,128]{2,1,0:T(8,128)(2,1)S(1)}) custom-call(bf16[16,16,128]{2,1,0:T(8,128)(2,1)S(1)} %collective-permute-done.other_ref, f32[4,128,128]{2,1,0:T(8,128)S(1)} %get-tuple-element.35.term_ref, bf16[256,256]{1,0:T(8,128)(2,1)S(1)} %get-tuple-element.36.wo_ref, ...), custom_call_target="tpu_custom_call" | custom-call | tf_op jit(solution)/shard_map/pallas_call | solution.py:316
  24.0 13.2 %all_to_all.10.recv_ref = bf16[16,64,128]{2,1,0:T(8,128)(2,1)S(1)} all-to-all(bf16[16,64,128]{2,1,0:T(8,128)(2,1)S(1)} %get-tuple-element.48), channel_id=1, replica_groups=mesh['dp'=2,'head'=1,'row'=16] {'row'}, dimensions={0} | all-to-all | bytes 524288 | tf_op jit(solution)/shard_map/all_to_all | solution.py:332
  37.2 0.9 %shard_map.117 = (bf16[8,128,128]{2,1,0:T(8,128)(2,1)}, bf16[8,64,128]{2,1,0:T(8,128)(2,1)}) custom-call(bf16[16,64,128]{2,1,0:T(8,128)(2,1)S(1)} %all_to_all.10.recv_ref, bf16[8,64,128]{2,1,0:T(8,128)(2,1)S(1)} %get-tuple-element.49.mirror_ref, bf16[64,128]{1,0:T(8,128)(2,1)S(1)} %get-tuple-element.37.wd_ref, f32[64,128]{1,0:T(8,128)S(1)} %get-tuple-element.38.db_ref), custom_call_target="tpu_custom_call" | custom-call | tf_op jit(solution)/shard_map/pallas_call | solution.py:316
  (3 shorter events, 0.0 us)
Async XLA Ops:
  2.8 7.6 %copy-start = (bf16[128,4,128]{2,1,0:T(4,128)(2,1)S(1)}, bf16[128,4,128]{2,1,0:T(4,128)(2,1)}, u32[]{:S(2)}) copy-start(bf16[128,4,128]{2,1,0:T(4,128)(2,1)} %w_ref.1) | copy-start | bytes 393220
  2.8 7.6 %copy-start.1 = (bf16[4,32,128]{2,1,0:T(8,128)(2,1)S(1)}, bf16[4,32,128]{2,1,0:T(8,128)(2,1)}, u32[]{:S(2)}) copy-start(bf16[4,32,128]{2,1,0:T(8,128)(2,1)} %param.17) | copy-start | bytes 98308
  2.8 7.6 %copy-start.2 = (bf16[128,64]{0,1:T(8,128)(2,1)S(1)}, bf16[128,64]{0,1:T(8,128)(2,1)}, u32[]{:S(2)}) copy-start(bf16[128,64]{0,1:T(8,128)(2,1)} %param.18) | copy-start | bytes 49156
  2.8 7.6 %copy-start.5 = (s32[128]{0:T(128)S(1)}, s32[128]{0:T(128)}, u32[]{:S(2)}) copy-start(s32[128]{0:T(128)} %param.11) | copy-start | bytes 1540
  2.8 7.6 %copy-start.6 = (s32[128]{0:T(128)S(1)}, s32[128]{0:T(128)}, u32[]{:S(2)}) copy-start(s32[128]{0:T(128)} %param.12) | copy-start | bytes 1540
  2.9 7.6 %copy-start.7 = (f32[64]{0:T(128)S(1)}, f32[64]{0:T(128)}, u32[]{:S(2)}) copy-start(f32[64]{0:T(128)} %param.19) | copy-start | bytes 772
  2.9 18.6 %all-to-all-start = ((bf16[16,80,128]{2,1,0:T(8,128)(2,1)}), bf16[16,80,128]{2,1,0:T(8,128)(2,1)S(1)}, u32[]{:S(2)}, u32[]{:S(2)}) async-start(bf16[16,80,128]{2,1,0:T(8,128)(2,1)} %shard_map.113), calls=%async_computation | async-start | bytes 655360 | tf_op jit(solution)/shard_map/all_to_all | solution.py:332
  10.4 0.7 %copy-start.3 = (f32[128]{0:T(128)S(1)}, f32[128]{0:T(128)}, u32[]{:S(2)}) copy-start(f32[128]{0:T(128)} %param.13) | copy-start | bytes 1540
  10.4 0.7 %copy-start.4 = (f32[2,4]{1,0:T(2,128)S(1)}, f32[2,4]{1,0:T(2,128)}, u32[]{:S(2)}) copy-start(f32[2,4]{1,0:T(2,128)} %cb_ref.1) | copy-start | bytes 100
  21.5 1.3 %collective-permute-start = (bf16[16,16,128]{2,1,0:T(8,128)(2,1)S(1)}, bf16[16,16,128]{2,1,0:T(8,128)(2,1)S(1)}, u32[]{:S(2)}, u32[]{:S(2)}) collective-permute-start(bf16[16,16,128]{2,1,0:T(8,128)(2,1)S(1)} %slice.3), channel_id=1, source_target_pairs={{0,1},{1,0},{2,3},{3,2},{4,5},{5,4},{6,7},{7,6},{8,9},{9,8},{10,11... | collective-permute-start | bytes 196616 | tf_op jit(solution)/shard_map/ppermute | solution.py:328
